TPU v7x, 128 devices: a whole 4x4x4 slice. The times are simulated.
128 devices in a mesh: seq: 8 (over z_hi, x), tp: 16 (over z_lo, y, core).
Axes of the slice: x: 4, y: 4, z: 4 (z_hi: 2, z_lo: 2; z = z_hi * 2 + z_lo), core: 2. Of those that a mesh axis runs over, the one named last changes fastest.
Arguments:
- rollout_acts: bfloat16 [2048, 8192], P('seq', 'tp'), may hold values from -6 to 6
- rollout_grads: bfloat16 [2048, 8192], P('seq', 'tp'), may hold values from -6 to 6
- lengths: int32 [8, 16], P('seq'), may hold values from 1 to 15, as said below
- destination: int32 [8, 16], P('seq'), may hold values from 0 to 7, as said below
- valid_mask: int32 [2048], P('seq'), may hold values 0 or 1
- advantage: float32 [8, 16], P('seq'), may hold values from -4 to 4
- gate_weight: bfloat16 [8192, 15360], P('tp', 'seq'), may hold values from -0.0625 to 0.0625
- up_weight: bfloat16 [8192, 15360], P('tp', 'seq'), may hold values from -0.0625 to 0.0625
- down_weight: bfloat16 [15360, 8192], P('seq', 'tp'), may hold values from -0.046875 to 0.046875
Outputs:
- block_out: bfloat16 [1024, 8192], P('seq', 'tp')
- input_grad: bfloat16 [1024, 8192], P('seq', 'tp')
- gate_grad: float32 [8192, 15360], P('tp', 'seq')
- up_grad: float32 [8192, 15360], P('tp', 'seq')
- down_grad: float32 [15360, 8192], P('seq', 'tp')
Inputs may be any that keep to these rules, and one draw needn't show every extreme that they name: `destination`: in each row every learner shard appears exactly 2 times. The lengths of the responses that one rollout device sends to one learner shard sum to at most 16; in every draw one learner shard receives exactly 16 tokens from every rollout device.
All inputs are finite; a program needn't handle non-finite values. No bound on the sum of `valid_mask` on one device may be relied on, other than what follows from the above.
Results may differ from a plain program's by a relative error of at most 0.0057.
Values may be sent and summed in bfloat16 or wider, within the bound.
A program may use at most 192 MiB of HBM per device.

v0:
```python
import jax
import jax.numpy as jnp
from jax import lax
from jax.sharding import PartitionSpec as P

BIN = 16


def width_sum(term, part_rows):
    return lax.psum_scatter(
        term(jnp.int32(0), part_rows * lax.axis_size("tp")), "tp", scatter_dimension=0, tiled=True
    )


def spread_middle(block):
    return lax.all_gather(block, "tp", axis=0, tiled=True)


def row_sum(term, part_rows):
    return lax.psum_scatter(
        term(jnp.int32(0), part_rows * lax.axis_size("seq")), "seq", scatter_dimension=0, tiled=True
    )


def per_device(
    rollout_acts,
    rollout_grads,
    lengths,
    destination,
    valid_mask,
    advantage,
    gate_weight,
    up_weight,
    down_weight,
):
    seq_count = lax.axis_size("seq")
    tp_count = lax.axis_size("tp")
    columns = rollout_acts.shape[1]
    resp_count = lengths.shape[1]
    own_lengths = lengths[0]
    own_dest = destination[0]
    order = jnp.arange(resp_count)
    same = own_dest[:, None] == own_dest[None, :]
    earlier = order[None, :] < order[:, None]
    offsets = jnp.sum(jnp.where(same & earlier, own_lengths[None, :], 0), axis=1)
    within = jnp.arange(BIN)
    target = own_dest[:, None] * BIN + offsets[:, None] + within[None, :]
    live = within[None, :] < own_lengths[:, None]
    dump_row = seq_count * BIN
    target = jnp.where(live, target, dump_row).reshape(-1)
    row_weight = jnp.repeat(advantage[0], BIN) * valid_mask.astype(jnp.float32)
    scaled = (rollout_grads.astype(jnp.float32) * row_weight[:, None]).astype(jnp.bfloat16)
    holder = jnp.zeros((dump_row + 1, columns), jnp.bfloat16)
    packed_acts = holder.at[target].set(rollout_acts)[:dump_row].reshape(seq_count, BIN, columns)
    packed_grads = holder.at[target].set(scaled)[:dump_row].reshape(seq_count, BIN, columns)
    arrived = (
        lax.all_to_all(packed_acts, "seq", split_axis=0, concat_axis=0, tiled=True),
        lax.all_to_all(packed_grads, "seq", split_axis=0, concat_axis=0, tiled=True),
    )
    learner = (arrived[0].reshape(-1, columns), arrived[1].reshape(-1, columns))
    all_acts, all_grads = (
        lax.all_gather(learner[0], "seq", axis=0, tiled=True),
        lax.all_gather(learner[1], "seq", axis=0, tiled=True),
    )
    total_rows = all_acts.shape[0]
    middle_rows = total_rows // tp_count
    learn_rows = total_rows // seq_count
    widths = gate_weight.shape[1]
    paired = jnp.concatenate([gate_weight, up_weight], axis=1)

    def gate_term(first_row, row_count):
        return jnp.dot(all_acts, paired, preferred_element_type=jnp.float32)

    gate_up = width_sum(gate_term, middle_rows)
    gate = gate_up[:, :widths]
    upper = gate_up[:, widths:]
    sigma = jax.nn.sigmoid(gate)
    hidden_part = (gate * sigma * upper).astype(jnp.bfloat16)
    hidden = spread_middle(hidden_part)

    def out_term(first_row, row_count):
        return jnp.dot(hidden, down_weight, preferred_element_type=jnp.float32)

    block_out = row_sum(out_term, learn_rows).astype(jnp.bfloat16)

    def back_term(first_row, row_count):
        return lax.dot_general(
            all_grads, down_weight, (((1,), (1,)), ((), ())), preferred_element_type=jnp.float32
        )

    grad_hidden = width_sum(back_term, middle_rows)
    grad_gate = grad_hidden * upper * sigma * (1.0 + gate * (1.0 - sigma))
    grad_upper = grad_hidden * gate * sigma
    grad_part = jnp.concatenate([grad_gate, grad_upper], axis=1).astype(jnp.bfloat16)
    grad_pre = spread_middle(grad_part)

    def input_term(first_row, row_count):
        return lax.dot_general(
            grad_pre, paired, (((1,), (1,)), ((), ())), preferred_element_type=jnp.float32
        )

    input_grad = row_sum(input_term, learn_rows).astype(jnp.bfloat16)
    grad_scale = 1.0 / jnp.sqrt(jnp.float32(total_rows))
    pair_grad = (
        lax.dot_general(
            all_acts, grad_pre, (((0,), (0,)), ((), ())), preferred_element_type=jnp.float32
        )
        * grad_scale
    )
    down_grad = (
        lax.dot_general(
            hidden, all_grads, (((0,), (0,)), ((), ())), preferred_element_type=jnp.float32
        )
        * grad_scale
    )
    return (block_out, input_grad, pair_grad[:, :widths], pair_grad[:, widths:], down_grad)


def solution(mesh):
    return jax.shard_map(
        per_device,
        mesh=mesh,
        in_specs=(
            P("seq", "tp"),
            P("seq", "tp"),
            P("seq", None),
            P("seq", None),
            P("seq"),
            P("seq", None),
            P("tp", "seq"),
            P("tp", "seq"),
            P("seq", "tp"),
        ),
        out_specs=(P("seq", "tp"), P("seq", "tp"), P("tp", "seq"), P("tp", "seq"), P("seq", "tp")),
        check_vma=False,
    )
```

profile of v0, /device:TPU:0, one launch (start us, length us, event | category | flops | bytes accessed | tf_op | source)
XLA Modules:
  0.0 548.7 jit_solution(12694346007265937455)
XLA Ops:
  7.2 1.0 select_reduce_fusion
  8.2 0.7 multiply_add_fusion
  8.9 0.7 add_select_fusion
  9.6 0.1 select_n.32
  9.7 0.7 broadcast_in_dim.34
  10.5 0.7 convert_multiply_fusion
  11.2 2.0 scatter_custom_fusion.1
  13.2 15.7 %all_to_all.10 = bf16[8,16,512]{2,1,0:T(8,128)(2,1)} all-to-all(bf16[8,16,512]{2,1,0:T(8,128)(2,1)S(1)} %bitcast.25), channel_id=1, replica_groups=mesh['seq'=8,'tp'=16] {'seq'}, dimensions={0} | all-to-all | bytes 262144 | tf_op jit(solution)/shard_map/all_to_all | solution.py:58
  28.9 1.9 scatter_custom_fusion
  30.9 11.2 %all_to_all.11 = bf16[8,16,512]{2,1,0:T(8,128)(2,1)} all-to-all(bf16[8,16,512]{2,1,0:T(8,128)(2,1)S(1)} %bitcast.26), channel_id=1, replica_groups=mesh['seq'=8,'tp'=16] {'seq'}, dimensions={0} | all-to-all | bytes 262144 | tf_op jit(solution)/shard_map/all_to_all | solution.py:57
  42.1 31.9 %all-gather.9.cloned.1.call-done = bf16[1024,512]{1,0:T(8,128)(2,1)} async-done(((bf16[128,512]{1,0:T(8,128)(2,1)}), bf16[1024,512]{1,0:T(8,128)(2,1)}) %all-gather.9.cloned.1.call-update) | async-done | bytes 1048592 | tf_op jit(solution)/shard_map/all_gather | solution.py:63
  74.0 6.7 %fusion.9 = f32[1024,1920]{1,0:T(8,128)} fusion(bf16[1024,512]{1,0:T(8,128)(2,1)} %all-gather.9.cloned.1.call-done, bf16[1920,512]{1,0:T(8,128)(2,1)S(1)} %copy-done), kind=kOutput, calls=%fused_computation.28 | convolution fusion | flops 2013265920 | bytes 10878976 | tf_op jit(solution)/shard_map/dot_general | solution.py:87
  80.9 3.1 constant_dynamic-update-slice_fusion.1
  84.0 1.4 constant_dynamic-update-slice_fusion
  85.4 37.1 %all-gather.5.cloned.1.call-done = bf16[1024,512]{1,0:T(8,128)(2,1)} async-done(((bf16[128,512]{1,0:T(8,128)(2,1)}), bf16[1024,512]{1,0:T(8,128)(2,1)}) %all-gather.5.cloned.1.call-update) | async-done | bytes 1048592 | tf_op jit(solution)/shard_map/all_gather | solution.py:62
  122.5 12.2 %fusion.7 = f32[1024,3840]{1,0:T(8,128)} fusion(bf16[1024,512]{1,0:T(8,128)(2,1)} %all-gather.5.cloned.1.call-done, bf16[512,3840]{1,0:T(8,128)(2,1)} %constant_dynamic-update-slice_fusion), kind=kOutput, calls=%fused_computation.26 | convolution fusion | flops 4026531840 | bytes 20709376 | tf_op jit(solution)/shard_map/dot_general | solution.py:72
  134.8 62.6 %reduce-scatter.9.cloned.1.call-done = f32[64,1920]{1,0:T(8,128)} async-done(((f32[1024,1920]{1,0:T(8,128)}), f32[64,1920]{1,0:T(8,128)}) %reduce-scatter.9.cloned.1.call-update) | async-done | bytes 491536 | tf_op jit(solution)/shard_map/reduce_scatter | solution.py:10
  197.4 93.9 %reduce-scatter.5.cloned.1.call-done = f32[64,3840]{1,0:T(8,128)} async-done(((f32[1024,3840]{1,0:T(8,128)}), f32[64,3840]{1,0:T(8,128)}) %reduce-scatter.5.cloned.1.call-update) | async-done | bytes 983056 | tf_op jit(solution)/shard_map/reduce_scatter | solution.py:10
  291.3 2.3 multiply_convert_fusion.2
  293.7 0.8 pad_maximum_fusion
  294.6 35.0 %all-gather.7.cloned.1.call-done = bf16[1024,1920]{1,0:T(8,128)(2,1)} async-done(((bf16[64,1920]{1,0:T(8,128)(2,1)}), bf16[1024,1920]{1,0:T(8,128)(2,1)}) %all-gather.7.cloned.1.call-update) | async-done | bytes 3932176 | tf_op jit(solution)/shard_map/all_gather | solution.py:16
  329.6 5.8 %fusion.8 = f32[1024,512]{1,0:T(8,128)} fusion(bf16[1024,1920]{1,0:T(8,128)(2,1)} %all-gather.7.cloned.1.call-done, bf16[1920,512]{1,0:T(8,128)(2,1)S(1)} %copy-done), kind=kOutput, calls=%fused_computation.27 | convolution fusion | flops 2013265920 | bytes 7995392 | tf_op jit(solution)/shard_map/dot_general | solution.py:82
  335.4 0.2 reduce-scatter.11.cloned.1.call-start
  335.6 45.9 %all-gather.11.cloned.1.call-done = bf16[1024,3840]{1,0:T(8,128)(2,1)} async-done(((bf16[64,3840]{1,0:T(8,128)(2,1)}), bf16[1024,3840]{1,0:T(8,128)(2,1)}) %all-gather.11.cloned.1.call-update) | async-done | bytes 7864336 | tf_op jit(solution)/shard_map/all_gather | solution.py:16
  381.5 10.0 %fusion.10 = f32[1024,512]{1,0:T(8,128)} fusion(bf16[1024,3840]{1,0:T(8,128)(2,1)} %all-gather.11.cloned.1.call-done, bf16[512,3840]{1,0:T(8,128)(2,1)} %constant_dynamic-update-slice_fusion), kind=kOutput, calls=%fused_computation.29 | convolution fusion | flops 4026531840 | bytes 13893632 | tf_op jit(solution)/shard_map/dot_general | solution.py:98
  391.5 6.4 %convolution_multiply_fusion.1 = f32[1920,512]{1,0:T(8,128)} fusion(bf16[1024,1920]{1,0:T(8,128)(2,1)} %all-gather.7.cloned.1.call-done, bf16[1024,512]{1,0:T(8,128)(2,1)S(1)} %copy-done.4), kind=kOutput, calls=%fused_computation.3 | convolution fusion | flops 2014248960 | bytes 8912896 | tf_op jit(solution)/shard_map/dot_general | solution.py:111
  397.9 64.2 %reduce-scatter.7.cloned.1.call-done = f32[128,512]{1,0:T(8,128)} async-done(((f32[1024,512]{1,0:T(8,128)}), f32[128,512]{1,0:T(8,128)}) %reduce-scatter.7.cloned.1.call-update) | async-done | bytes 262160 | tf_op jit(solution)/shard_map/reduce_scatter | solution.py:20
  462.1 1.6 convert_element_type.20
  463.8 6.6 %convolution_multiply_fusion = f32[512,3840]{1,0:T(8,128)S(1)} fusion(bf16[1024,512]{1,0:T(8,128)(2,1)S(1)} %copy-done.3, bf16[1024,3840]{1,0:T(8,128)(2,1)} %all-gather.11.cloned.1.call-done), kind=kOutput, calls=%fused_computation.2 | convolution fusion | flops 4028497920 | bytes 16777216 | tf_op jit(solution)/shard_map/dot_general | solution.py:105
  470.4 3.7 fusion.6
  474.1 66.2 %reduce-scatter.11.cloned.1.call-done = f32[128,512]{1,0:T(8,128)} async-done(((f32[1024,512]{1,0:T(8,128)}), f32[128,512]{1,0:T(8,128)}) %reduce-scatter.11.cloned.1.call-update) | async-done | bytes 262160 | tf_op jit(solution)/shard_map/reduce_scatter | solution.py:20
  540.3 1.6 convert_element_type.24
  (29 shorter events, 0.6 us)
Async XLA Ops:
  7.2 66.9 %copy-start = (bf16[1920,512]{1,0:T(8,128)(2,1)S(1)}, bf16[1920,512]{1,0:T(8,128)(2,1)}, u32[]{:S(2)}) copy-start(bf16[1920,512]{1,0:T(8,128)(2,1)} %param.17) | copy-start | bytes 5898244
  7.2 66.9 %all-gather.9.cloned.1.call-start = ((), (), s32[]{:S(2)}) async-start(), calls=%async_computation.10 | async-start | bytes 1179648 | tf_op jit(solution)/shard_map/all_gather | solution.py:63
  28.9 93.6 %all-gather.5.cloned.1.call-start = ((), (), s32[]{:S(2)}) async-start(), calls=%async_computation.6 | async-start | bytes 1179648 | tf_op jit(solution)/shard_map/all_gather | solution.py:62
  42.0 155.4 %reduce-scatter.9.cloned.1.call-start = ((), (), s32[]{:S(2)}) async-start(), calls=%async_computation.11 | async-start | bytes 8355840 | tf_op jit(solution)/shard_map/reduce_scatter | solution.py:10
  80.8 210.5 %reduce-scatter.5.cloned.1.call-start = ((), (), s32[]{:S(2)}) async-start(), calls=%async_computation.7 | async-start | bytes 16711680 | tf_op jit(solution)/shard_map/reduce_scatter | solution.py:10
  80.9 3.1 copy-start.2
  134.7 194.8 %all-gather.7.cloned.1.call-start = ((), (), s32[]{:S(2)}) async-start(), calls=%async_computation.8 | async-start | bytes 4177920 | tf_op jit(solution)/shard_map/all_gather | solution.py:16
  293.6 87.8 %all-gather.11.cloned.1.call-start = ((), (), s32[]{:S(2)}) async-start(), calls=%async_computation.12 | async-start | bytes 8355840 | tf_op jit(solution)/shard_map/all_gather | solution.py:16
  294.5 167.6 %reduce-scatter.7.cloned.1.call-start = ((), (), s32[]{:S(2)}) async-start(), calls=%async_computation.9 | async-start | bytes 2359296 | tf_op jit(solution)/shard_map/reduce_scatter | solution.py:20
  335.4 56.2 %copy-start.4 = (bf16[1024,512]{1,0:T(8,128)(2,1)S(1)}, bf16[1024,512]{1,0:T(8,128)(2,1)}, u32[]{:S(2)}) copy-start(bf16[1024,512]{1,0:T(8,128)(2,1)} %all-gather.9.cloned.1.call-done) | copy-start | bytes 3145732
  335.4 204.9 %reduce-scatter.11.cloned.1.call-start = ((), (), s32[]{:S(2)}) async-start(), calls=%async_computation.13 | async-start | bytes 2359296 | tf_op jit(solution)/shard_map/reduce_scatter | solution.py:20
  391.5 72.2 %copy-start.3 = (bf16[1024,512]{1,0:T(8,128)(2,1)S(1)}, bf16[1024,512]{1,0:T(8,128)(2,1)}, u32[]{:S(2)}) copy-start(bf16[1024,512]{1,0:T(8,128)(2,1)} %all-gather.5.cloned.1.call-done) | copy-start | bytes 3145732
  470.4 71.5 %copy-start.1 = (bf16[1920,512]{1,0:T(8,128)(2,1)S(1)}, bf16[1920,512]{1,0:T(8,128)(2,1)}, u32[]{:S(2)}) copy-start(bf16[1920,512]{1,0:T(8,128)(2,1)} %param.17) | copy-start | bytes 5898244
Sparse Core Ops, SparseCore 0:
  29.0 44.9 all-gather.8
  76.4 46.0 all-gather.4
  124.9 72.4 reduce-scatter.8
  199.7 91.5 reduce-scatter.4
  293.8 35.7 all-gather.6
  331.7 49.7 all-gather.10
  385.8 76.2 reduce-scatter.6
  466.4 73.8 reduce-scatter.10
where the time goes:
time: 549 us
  waiting for transfers between devices  437 us (80%)
  matrix products  47.7 us (9%)
  blocking collectives  26.8 us (5%)
  between operations  14.2 us (3%)
  other arithmetic  11.4 us (2%)
  local copies, waits for them, and re-layouts  11.1 us (2%)
    reduce_scatter x2, waiting for transfers between devices, width_sum(): lax.psum_scatter(term(jnp.int32(0), part_rows * lax.axis_size('tp')), 'tp...  157 us
    reduce_scatter x2, waiting for transfers between devices, row_sum(): lax.psum_scatter(term(jnp.int32(0), part_rows * lax.axis_size('seq')), 's...  130 us
    all_gather x2, waiting for transfers between devices, spread_middle(): return lax.all_gather(block, 'tp', axis=0, tiled=True)  80.9 us
    all_gather x1, waiting for transfers between devices, per_device(): lax.all_gather(learner[0], 'seq', axis=0, tiled=True)  37.1 us
    all_gather x1, waiting for transfers between devices, per_device(): lax.all_gather(learner[1], 'seq', axis=0, tiled=True)  31.9 us
    all_to_all x1, blocking collectives, per_device(): lax.all_to_all(packed_grads, 'seq', split_axis=0, concat_axis=0, tiled=True)  15.7 us
    dot_general x1, matrix products, gate_term(): return jnp.dot(all_acts, paired, preferred_element_type=jnp.float32)  12.2 us
    all_to_all x1, blocking collectives, per_device(): lax.all_to_all(packed_acts, 'seq', split_axis=0, concat_axis=0, tiled=True)  11.2 us
  transfers between devices with their start and end apart: 8, of which 8 were waited for; matrix products, arithmetic and copies ran while one was open for 11% of the time, Pallas kernels for 0%

commit v1 on v0

v1 whole, which is shorter than its diff:
```python
import jax
import jax.numpy as jnp
from jax import lax
from jax.experimental import pallas as pl
from jax.experimental.pallas import tpu as pltpu
from jax.sharding import PartitionSpec as P

BIN = 16
NC = 4
WIDTH = 512
HID = 1920
ALL = 3 * HID
CY = 3200
CZ = ALL - CY
HZ = CZ // 2
UNIT = 640
BF = jnp.bfloat16
F32 = jnp.float32
MESH = pl.DeviceIdType.MESH

SEQ_NAMES = ["zh", "xo+", "xo-", "xp+", "xp-", "xf+", "xf-"]
W_NAMES = ["wg", "wu", "wd"]
CHUNK_NAMES = [
    "q",
    "y1+", "y1-", "yo+", "yo-", "ya+", "ya-", "yz",
    "z1", "r1+", "r1-", "ro+", "ro-", "ra+", "ra-",
    "az", "ay+", "ay-", "by+", "by-", "bz0", "ap+", "ap-", "bf+", "bf-",
    "bz1", "bz2", "af+", "af-", "bz3", "core",
]
SEM = {}
for _n in SEQ_NAMES + W_NAMES:
    SEM[(_n, 0)] = len(SEM)
for _k in range(NC):
    for _n in CHUNK_NAMES:
        SEM[(_n, _k)] = len(SEM)
N_SEM = len(SEM)

YCOL = pl.ds(0, CY)
ZCOL = pl.ds(CY, CZ)
ZCOL_A = pl.ds(CY, HZ)
ZCOL_B = pl.ds(CY + HZ, HZ)


def up32(value):
    return value.astype(F32)


def mega(
    acts_ref, grads_ref, hot_ref, weight_ref, gate_hbm, up_hbm, down_hbm,
    hid_out, gg_out, gu_out, acts_out, grads_out,
    wg, wu, wd, pg, pu, pd, G, Q, PP, H,
    y1, yown, yacc, ysend, yz, z1, r1, rown, racc, F,
    ssem, rsem, lsem,
):
    s = lax.axis_index("seq")
    t = lax.axis_index("tp")
    zh, x = s // 4, lax.rem(s, 4)
    zl, y, c = t // 8, lax.rem(t // 2, 4), lax.rem(t, 2)
    oz, oc, oh = 1 - zl, 1 - c, 1 - zh
    yp, ym, y2 = lax.rem(y + 1, 4), lax.rem(y + 3, 4), lax.rem(y + 2, 4)

    def dev(zh_=zh, x_=x, zl_=zl, y_=y, c_=c):
        return (zh_ * 4 + x_, zl_ * 8 + y_ * 2 + c_)

    XP, XM = dev(x_=lax.rem(x + 1, 4)), dev(x_=lax.rem(x + 3, 4))
    YP, YM = dev(y_=yp), dev(y_=ym)
    ZL, ZH, CO = dev(zl_=oz), dev(zh_=oh), dev(c_=oc)

    copies = {}

    def send(name, k, src, dst, to):
        i = SEM[(name, k)]
        cp = pltpu.make_async_remote_copy(
            src_ref=src, dst_ref=dst, send_sem=ssem.at[i], recv_sem=rsem.at[i],
            device_id=to, device_id_type=MESH,
        )
        cp.start()
        copies[(name, k)] = cp

    def recv(name, k):
        copies[(name, k)].wait_recv()

    local = []

    def local_copy(src, dst):
        cp = pltpu.make_async_copy(src, dst, lsem.at[len(local)])
        cp.start()
        local.append(cp)
        return cp

    loads = [local_copy(gate_hbm, wg), local_copy(up_hbm, wu), local_copy(down_hbm, wd)]
    barrier = pltpu.get_barrier_semaphore()
    for peer in (XP, XM, YP, YM, ZL, ZH, CO):
        pl.semaphore_signal(barrier, inc=1, device_id=peer, device_id_type=MESH)

    hot = hot_ref[...]
    G[0, 0, zh] = jnp.dot(hot, acts_ref[...], preferred_element_type=F32).astype(BF)
    scaled = (up32(grads_ref[...]) * weight_ref[...]).astype(BF)
    G[1, 0, zh] = jnp.dot(hot, scaled, preferred_element_type=F32).astype(BF)

    pl.semaphore_wait(barrier, 7)

    send("zh", 0, G.at[:, 0, zh], G.at[:, 0, zh], ZH)
    send("xo+", 0, G.at[:, 0, zh], G.at[:, 1, zh], XP)
    send("xo-", 0, G.at[:, 0, zh], G.at[:, 2, zh], XM)
    for cp, name, src, dst in zip(loads, W_NAMES, (wg, wu, wd), (pg, pu, pd)):
        cp.wait()
        send(name, 0, src, dst, CO)
    recv("zh", 0)
    send("q", 0, G.at[:, 0, oc], Q.at[:, 0], CO)
    send("xp+", 0, G.at[:, 0, oh], G.at[:, 1, oh], XP)
    send("xp-", 0, G.at[:, 0, oh], G.at[:, 2, oh], XM)

    def forward(k):
        recv("q", k)
        a_own, a_par = G[0, k, c], Q[0, k]
        for own, par, first in ((wg, pg, 0), (wu, pu, HID)):
            def unit(u, carry, own=own, par=par, first=first):
                cols = pl.ds(pl.multiple_of(u * UNIT, 128), UNIT)
                to = pl.ds(pl.multiple_of(u * UNIT + first, 128), UNIT)
                part = jnp.dot(a_own, own[:, cols], preferred_element_type=F32)
                part += jnp.dot(a_par, par[:, cols], preferred_element_type=F32)
                PP[k, :, :, to] = part.astype(BF).reshape(8, BIN, UNIT)
                return carry
            lax.fori_loop(0, 3, unit, 0)
        send("y1+", k, PP.at[k, y2, :, YCOL], y1.at[k, 0], YP)
        send("y1-", k, PP.at[k, 4 + y2, :, YCOL], y1.at[k, 1], YM)
        send("yo+", k, PP.at[k, 4 + yp, :, YCOL], yown.at[k, 1], YP)
        send("yo-", k, PP.at[k, ym, :, YCOL], yown.at[k, 0], YM)
        g_own, g_par = G[1, k, c], Q[1, k]

        def unit_back(u, carry):
            rows = pl.ds(pl.multiple_of(u * UNIT, 128), UNIT)
            to = pl.ds(pl.multiple_of(u * UNIT + 2 * HID, 128), UNIT)
            nt = (((1,), (1,)), ((), ()))
            part = lax.dot_general(g_own, wd[rows, :], nt, preferred_element_type=F32)
            part += lax.dot_general(g_par, pd[rows, :], nt, preferred_element_type=F32)
            PP[k, :, :, to] = part.astype(BF).reshape(8, BIN, UNIT)
            return carry
        lax.fori_loop(0, 3, unit_back, 0)
        send("z1", k, PP.at[k, pl.ds(oz * 4, 4), :, ZCOL], z1.at[k], ZL)

    def reduce_one(k):
        recv("y1+", k)
        y1[k, 0] = (up32(y1[k, 0]) + up32(PP[k, yp, :, YCOL])).astype(BF)
        send("ya+", k, y1.at[k, 0], yacc.at[k, 0], YP)
        recv("y1-", k)
        y1[k, 1] = (up32(y1[k, 1]) + up32(PP[k, 4 + ym, :, YCOL])).astype(BF)
        send("ya-", k, y1.at[k, 1], yacc.at[k, 1], YM)
        recv("z1", k)
        for row in (y2, yp, ym):
            z1[k, row] = (up32(z1[k, row]) + up32(PP[k, zl * 4 + row, :, ZCOL])).astype(BF)
        send("r1+", k, z1.at[k, y2, :, pl.ds(0, HZ)], r1.at[k, 0], YP)
        send("r1-", k, z1.at[k, y2, :, pl.ds(HZ, HZ)], r1.at[k, 1], YM)
        send("ro+", k, z1.at[k, yp, :, pl.ds(HZ, HZ)], rown.at[k, 1], YP)
        send("ro-", k, z1.at[k, ym, :, pl.ds(0, HZ)], rown.at[k, 0], YM)

    def reduce_two(k):
        for name in ("yo+", "yo-", "ya+", "ya-"):
            recv(name, k)
        ysend[k] = (
            up32(PP[k, oz * 4 + y, :, YCOL]) + up32(yacc[k, oz]) + up32(yown[k, oz])
        ).astype(BF)
        send("yz", k, ysend.at[k], yz.at[k], ZL)
        recv("r1+", k)
        r1[k, 0] = (up32(r1[k, 0]) + up32(z1[k, yp, :, pl.ds(0, HZ)])).astype(BF)
        send("ra+", k, r1.at[k, 0], racc.at[k, 0], YP)
        recv("r1-", k)
        r1[k, 1] = (up32(r1[k, 1]) + up32(z1[k, ym, :, pl.ds(HZ, HZ)])).astype(BF)
        send("ra-", k, r1.at[k, 1], racc.at[k, 1], YM)

    def finish(k):
        for name in ("yz", "ro+", "ro-", "ra+", "ra-"):
            recv(name, k)
        mine = zl * 4 + y
        F[:, YCOL] = (
            up32(PP[k, mine, :, YCOL]) + up32(yacc[k, zl]) + up32(yown[k, zl]) + up32(yz[k])
        )
        for half, cols in ((0, ZCOL_A), (1, ZCOL_B)):
            F[:, cols] = (
                up32(PP[k, mine, :, cols]) + up32(z1[k, y, :, pl.ds(half * HZ, HZ)])
                + up32(racc[k, half]) + up32(rown[k, half])
            )
        gate, upper, back = F[:, :HID], F[:, HID:2 * HID], F[:, 2 * HID:]
        sigma = jax.nn.sigmoid(gate)
        swish = gate * sigma
        H[k, c, mine, :, :HID] = (swish * upper).astype(BF)
        H[k, c, mine, :, HID:2 * HID] = (
            back * upper * sigma * (1.0 + gate * (1.0 - sigma))
        ).astype(BF)
        H[k, c, mine, :, 2 * HID:] = (back * swish).astype(BF)
        a = H.at[k, c, mine, :, YCOL]
        b = H.at[k, c, mine, :, ZCOL]
        send("az", k, a, a, ZL)
        send("ay+", k, a, a, YP)
        send("ay-", k, a, a, YM)
        send("by+", k, b, b, YP)
        send("by-", k, b, b, YM)
        send("bz0", k, b, b, ZL)

    def gather_one(k):
        recv("by+", k)
        b = H.at[k, c, zl * 4 + ym, :, ZCOL_A]
        send("bf+", k, b, b, YP)
        b = H.at[k, c, zl * 4 + ym, :, ZCOL]
        send("bz1", k, b, b, ZL)
        recv("by-", k)
        b = H.at[k, c, zl * 4 + yp, :, ZCOL_B]
        send("bf-", k, b, b, YM)
        b = H.at[k, c, zl * 4 + yp, :, ZCOL]
        send("bz2", k, b, b, ZL)
        recv("az", k)
        a = H.at[k, c, oz * 4 + y, :, YCOL]
        send("ap+", k, a, a, YP)
        send("ap-", k, a, a, YM)
        recv("ay+", k)
        a = H.at[k, c, zl * 4 + ym, :, YCOL]
        send("af+", k, a, a, YP)
        recv("ay-", k)

    def gather_two(k):
        recv("bf+", k)
        recv("bf-", k)
        b = H.at[k, c, zl * 4 + y2, :, ZCOL]
        send("bz3", k, b, b, ZL)
        recv("ap+", k)
        recv("ap-", k)
        a = H.at[k, c, oz * 4 + yp, :, YCOL]
        send("af-", k, a, a, YM)

    def gather_three(k):
        for name in ("af+", "af-", "bz0", "bz1", "bz2", "bz3"):
            recv(name, k)
        send("core", k, H.at[k, c], H.at[k, c], CO)

    def last(k):
        recv("core", k)
        for first, out in ((0, hid_out), (HID, gg_out), (2 * HID, gu_out)):
            local_copy(H.at[k, :, :, :, pl.ds(first, HID)], out.at[k])

    def seq_one():
        for name in ("xo+", "xp+", "xo-", "xp-"):
            recv(name, 0)
        send("xf+", 0, G.at[:, 1, 0], G.at[:, 3, 0], XP)
        send("xf-", 0, G.at[:, 2, 1], G.at[:, 3, 1], XM)
        send("q", 1, G.at[:, 1, oc], Q.at[:, 1], CO)
        send("q", 2, G.at[:, 2, oc], Q.at[:, 2], CO)

    def seq_two():
        recv("xf+", 0)
        recv("xf-", 0)
        send("q", 3, G.at[:, 3, oc], Q.at[:, 3], CO)
        local_copy(G.at[0], acts_out)
        local_copy(G.at[1], grads_out)

    for name in W_NAMES:
        recv(name, 0)
    stages = [forward, reduce_one, reduce_two, finish, gather_one, gather_two, gather_three, last]
    for slot in range(NC + len(stages) - 1):
        if slot < NC:
            forward(slot)
        if slot == 0:
            seq_one()
        if slot == 2:
            seq_two()
        for k in range(NC):
            stage = slot - k
            if 1 <= stage < len(stages):
                stages[stage](k)
    for cp in copies.values():
        cp.wait_send()
    for cp in local[len(loads):]:
        cp.wait()


def run_mega(acts, grads, hot, weight, gate, up, down):
    vm = pltpu.VMEM
    shape = jax.ShapeDtypeStruct
    rows = shape((NC, 2, 8, BIN, HID), BF)
    packed = shape((NC, 2, 128, WIDTH), BF)
    return pl.pallas_call(
        mega,
        out_shape=(rows, rows, rows, packed, packed),
        in_specs=[pl.BlockSpec(memory_space=vm)] * 4 + [pl.BlockSpec(memory_space=pl.ANY)] * 3,
        out_specs=tuple([pl.BlockSpec(memory_space=pl.ANY)] * 5),
        scratch_shapes=[
            vm((WIDTH, HID), BF), vm((WIDTH, HID), BF), vm((HID, WIDTH), BF),
            vm((WIDTH, HID), BF), vm((WIDTH, HID), BF), vm((HID, WIDTH), BF),
            vm((2, NC, 2, 128, WIDTH), BF),
            vm((2, NC, 128, WIDTH), BF),
            vm((NC, 8, BIN, ALL), BF),
            vm((NC, 2, 8, BIN, ALL), BF),
            vm((NC, 2, BIN, CY), BF), vm((NC, 2, BIN, CY), BF), vm((NC, 2, BIN, CY), BF),
            vm((NC, BIN, CY), BF), vm((NC, BIN, CY), BF),
            vm((NC, 4, BIN, CZ), BF),
            vm((NC, 2, BIN, HZ), BF), vm((NC, 2, BIN, HZ), BF), vm((NC, 2, BIN, HZ), BF),
            vm((BIN, ALL), F32),
            pltpu.SemaphoreType.DMA((N_SEM,)),
            pltpu.SemaphoreType.DMA((N_SEM,)),
            pltpu.SemaphoreType.DMA((32,)),
        ],
        compiler_params=pltpu.CompilerParams(
            collective_id=0, has_side_effects=True, vmem_limit_bytes=60 * 2**20
        ),
        name="mega",
    )(acts, grads, hot, weight, gate, up, down)


def per_device(
    rollout_acts, rollout_grads, lengths, destination, valid_mask, advantage,
    gate_weight, up_weight, down_weight,
):
    x = lax.rem(lax.axis_index("seq"), 4)
    own_lengths = lengths[0]
    own_dest = destination[0]
    order = jnp.arange(own_dest.shape[0])
    same = own_dest[:, None] == own_dest[None, :]
    earlier = order[None, :] < order[:, None]
    offsets = jnp.sum(jnp.where(same & earlier, own_lengths[None, :], 0), axis=1)
    within = jnp.arange(BIN)
    target = own_dest[:, None] * BIN + offsets[:, None] + within[None, :]
    live = within[None, :] < own_lengths[:, None]
    target = jnp.where(live, target, -1).reshape(-1)
    hot = (jnp.arange(8 * BIN)[:, None] == target[None, :]).astype(BF)
    row_weight = jnp.repeat(advantage[0], BIN) * valid_mask.astype(F32)
    hidden, gg, gu, acts, grads = run_mega(
        rollout_acts, rollout_grads, hot, row_weight[:, None], gate_weight, up_weight, down_weight
    )
    total = 1024
    hidden, gg, gu = (v.reshape(total, HID) for v in (hidden, gg, gu))
    acts, grads = acts.reshape(total, WIDTH), grads.reshape(total, WIDTH)
    block = jnp.dot(hidden, down_weight, preferred_element_type=F32)
    nt = (((1,), (1,)), ((), ()))
    inner = lax.dot_general(gg, gate_weight, nt, preferred_element_type=F32)
    inner += lax.dot_general(gu, up_weight, nt, preferred_element_type=F32)
    both = jnp.concatenate([block, inner], axis=1).reshape(NC, 2, 8, BIN, 2 * WIDTH)
    chunk_of = jnp.array([0, 2, 3, 1])[lax.rem(jnp.arange(4) - x + 4, 4)]
    both = both[chunk_of]
    both = both.transpose(2, 1, 0, 3, 4).reshape(total, 2 * WIDTH)
    both = lax.psum_scatter(both, "seq", scatter_dimension=0, tiled=True).astype(BF)
    scale = 1.0 / jnp.sqrt(jnp.float32(total))
    tn = (((0,), (0,)), ((), ()))
    gate_grad = lax.dot_general(acts, gg, tn, preferred_element_type=F32) * scale
    up_grad = lax.dot_general(acts, gu, tn, preferred_element_type=F32) * scale
    down_grad = lax.dot_general(hidden, grads, tn, preferred_element_type=F32) * scale
    return both[:, :WIDTH], both[:, WIDTH:], gate_grad, up_grad, down_grad


def solution(mesh):
    return jax.shard_map(
        per_device,
        mesh=mesh,
        in_specs=(
            P("seq", "tp"), P("seq", "tp"), P("seq", None), P("seq", None), P("seq"),
            P("seq", None), P("tp", "seq"), P("tp", "seq"), P("seq", "tp"),
        ),
        out_specs=(P("seq", "tp"), P("seq", "tp"), P("tp", "seq"), P("tp", "seq"), P("seq", "tp")),
        check_vma=False,
    )
```

time: 549 us -> 243 us (0.44)
  waiting for transfers between devices: 437 us -> 68.9 us
  Pallas kernels: 0 us -> 107 us
  blocking collectives: 26.8 us -> 0 us
  matrix products: 47.7 us -> 24.5 us
  local copies, waits for them, and re-layouts: 11.1 us -> 20.3 us
    reduce_scatter x4 -> x1, waiting for transfers between devices: 287 us -> 68.9 us  [per_device(): lax.psum_scatter(both, 'seq', scatter_dimension=0, tiled=True).astype(BF)]
    all_gather x4 -> x0, waiting for transfers between devices: 150 us -> none  [the longest x2 80.9 us: spread_middle(): return lax.all_gather(block, 'tp', axis=0, tiled=True)]
    pallas_call x0 -> x1, Pallas kernels: none -> 107 us  [run_mega(): pl.pallas_call(mega, out_shape=(rows, rows, rows, packed, packed), in_spe...]
    all_to_all x2 -> x0, blocking collectives: 26.8 us -> none  [the longest x1 15.7 us: per_device(): lax.all_to_all(packed_grads, 'seq', split_axis=0, concat_axis=0, tiled=True)]
    dot_general x6, matrix products: 47.7 us -> 24.5 us  [the longest x1 6.55 us: per_device(): lax.dot_general(acts, gg, tn, preferred_element_type=F32) * scale]
    gather x0 -> x2, local copies, waits for them, and re-layouts: none -> 6.27 us  [the longest x1 4.98 us: per_device(): both = both[chunk_of]]
  transfers between devices with their start and end apart: 8 -> 1, of which waited for: 8 -> 1; matrix products, arithmetic and copies ran while one was open for 11% -> 6% of each run, Pallas kernels for 0% -> 0%
where the time goes in v1:
time: 243 us; the launch traced here: 242 us
  Pallas kernels  107 us (44%)
  waiting for transfers between devices  68.9 us (28%)
  matrix products  24.5 us (10%)
  local copies, waits for them, and re-layouts  20.3 us (8%)
  between operations  14.2 us (6%)
  other arithmetic  7.11 us (3%)
    pallas_call x1, Pallas kernels, run_mega(): pl.pallas_call(mega, out_shape=(rows, rows, rows, packed, packed), in_spe...  107 us
    reduce_scatter x1, waiting for transfers between devices, per_device(): lax.psum_scatter(both, 'seq', scatter_dimension=0, tiled=True).astype(BF)  68.9 us
    dot_general x1, matrix products, per_device(): lax.dot_general(acts, gg, tn, preferred_element_type=F32) * scale  6.55 us
    concatenate x1, local copies, waits for them, and re-layouts, per_device(): jnp.concatenate([block, inner], axis=1).reshape(NC, 2, 8, BIN, 2 * WIDTH)  5.35 us
    gather x1, local copies, waits for them, and re-layouts, per_device(): both = both[chunk_of]  4.98 us
  transfers between devices with their start and end apart: 1, of which 1 were waited for; matrix products, arithmetic and copies ran while one was open for 6% of the time, Pallas kernels for 0%

profile of v1, /device:TPU:0, one launch (start us, length us, event | category | flops | bytes accessed | tf_op | source)
XLA Modules:
  0.0 242.1 jit_solution(413576815807414120)
XLA Ops:
  7.2 0.0 copy-start.3
  7.2 0.0 reduce-scatter.2.cloned.1.call-start
  7.2 1.0 select_reduce_fusion
  8.2 0.7 multiply_add_fusion
  8.9 1.3 gather_fusion
  10.2 0.7 add_select_fusion
  10.9 0.1 select_n.37
  11.0 0.7 broadcast_in_dim.33
  11.8 0.1 reshape.128
  11.8 0.6 fusion.hot_ref
  12.5 0.7 convert_multiply_fusion
  13.2 0.8 copy.21.weight_ref
  14.0 107.2 %mega.1 = (bf16[4,2,8,16,1920]{4,3,2,1,0:T(8,128)(2,1)}, bf16[4,2,8,16,1920]{4,3,2,1,0:T(8,128)(2,1)}, bf16[4,2,8,16,1920]{4,3,2,1,0:T(8,128)(2,1)}, bf16[4,2,12...) custom-call(bf16[256,512]{1,0:T(8,128)(2,1)} %acts_ref.1, bf16[256,512]{1,0:T(8,128)(2,1)} %grads_ref.1, ...), custom_call_target="tpu_custom_call" | custom-call | tf_op jit(solution)/shard_map/mega/pallas_call | solution.py:281
  121.2 0.0 copy-start.4
  121.2 0.0 copy-start.6
  121.2 4.6 %fusion.7 = f32[1024,512]{0,1:T(8,128)S(1)} fusion(bf16[1024,1920]{1,0:T(8,128)(2,1)} %bitcast.38, bf16[512,1920]{1,0:T(8,128)(2,1)S(1)} %copy-done.3), kind=kOutput, calls=%fused_computation.27 | convolution fusion | flops 2013265920 | bytes 7995392 | tf_op jit(solution)/shard_map/dot_general | solution.py:334
  125.9 0.0 copy-start.5
  125.9 2.4 fusion.6
  128.3 0.3 copy-done.5
  128.6 2.4 convolution_add_fusion
  131.0 2.3 pad_maximum_fusion
  133.3 5.3 %copy.22 = f32[1024,1024]{1,0:T(8,128)} copy(f32[1024,1024]{0,1:T(8,128)} %pad_maximum_fusion) | data formatting | bytes 8388608 | tf_op jit(solution)/shard_map/concatenate | solution.py:336
  138.6 5.0 %gather_fusion.1 = f32[4,2,8,16,1024]{4,3,2,1,0:T(8,128)} fusion(f32[4,2,8,16,1024]{4,3,2,1,0:T(8,128)} %bitcast.32, s32[1024]{0:T(1024)S(1)} %pad_clamp_fusion), kind=kCustom, calls=%fused_computation.1 | custom fusion | bytes 8388624 | tf_op jit(solution)/shard_map/gather | solution.py:338
  143.6 4.7 %copy.23 = f32[8,2,4,16,1024]{4,3,2,1,0:T(8,128)} copy(f32[8,2,4,16,1024]{4,3,0,1,2:T(8,128)} %bitcast.33) | data formatting | bytes 8388608 | tf_op jit(solution)/shard_map/transpose | solution.py:339
  148.3 0.0 reduce-scatter.2.cloned.1.call-update
  148.3 1.2 copy-done
  149.5 6.6 %convolution_multiply_fusion.2 = f32[512,1920]{1,0:T(8,128)} fusion(bf16[1024,512]{1,0:T(8,128)(2,1)S(1)} %bitcast.34, bf16[1024,1920]{1,0:T(8,128)(2,1)} %bitcast.39), kind=kOutput, calls=%fused_computation.5 | convolution fusion | flops 2014248960 | bytes 8912896 | tf_op jit(solution)/shard_map/dot_general | solution.py:343
  156.1 4.3 %convolution_multiply_fusion.1 = f32[512,1920]{1,0:T(8,128)} fusion(bf16[1024,512]{1,0:T(8,128)(2,1)S(1)} %bitcast.35, bf16[1024,1920]{1,0:T(8,128)(2,1)S(1)} %bitcast.37), kind=kOutput, calls=%fused_computation.4 | convolution fusion | flops 2014248960 | bytes 8912896 | tf_op jit(solution)/shard_map/dot_general | solution.py:344
  160.4 4.2 %convolution_multiply_fusion = f32[1920,512]{1,0:T(8,128)} fusion(bf16[1024,1920]{1,0:T(8,128)(2,1)S(1)} %bitcast.46, bf16[1024,512]{1,0:T(8,128)(2,1)S(1)} %bitcast.47), kind=kOutput, calls=%fused_computation.3 | convolution fusion | flops 2014248960 | bytes 8912896 | tf_op jit(solution)/shard_map/dot_general | solution.py:345
  164.6 68.9 %reduce-scatter.2.cloned.1.call-done = f32[128,1024]{1,0:T(8,128)} async-done(((f32[1024,1024]{1,0:T(8,128)}), f32[128,1024]{1,0:T(8,128)}) %reduce-scatter.2.cloned.1.call-update) | async-done | bytes 524304 | tf_op jit(solution)/shard_map/reduce_scatter | solution.py:340
  233.5 1.1 convert_element_type.11
  234.6 0.7 fusion.5
  (16 shorter events, 0.1 us)
Async XLA Ops:
  7.2 114.0 %copy-start.3 = (bf16[512,1920]{1,0:T(8,128)(2,1)S(1)}, bf16[512,1920]{1,0:T(8,128)(2,1)}, u32[]{:S(2)}) copy-start(bf16[512,1920]{1,0:T(8,128)(2,1)} %gate_hbm.1) | copy-start | bytes 5898244
  7.2 226.3 %reduce-scatter.2.cloned.1.call-start = ((), (), s32[]{:S(2)}) async-start(), calls=%async_computation.1 | async-start | bytes 4718592 | tf_op jit(solution)/shard_map/reduce_scatter | solution.py:340
  121.2 4.6 %copy-start.4 = (bf16[1920,512]{1,0:T(8,128)(2,1)S(1)}, bf16[1920,512]{1,0:T(8,128)(2,1)}, u32[]{:S(2)}) copy-start(bf16[1920,512]{1,0:T(8,128)(2,1)} %down_hbm.1) | copy-start | bytes 5898244
  121.2 4.6 %copy-start.6 = (bf16[4,2,8,16,1920]{4,3,2,1,0:T(8,128)(2,1)S(1)}, bf16[4,2,8,16,1920]{4,3,2,1,0:T(8,128)(2,1)}, u32[]{:S(2)}) copy-start(bf16[4,2,8,16,1920]{4,3,2,1,0:T(8,128)(2,1)} %get-tuple-element.10) | copy-start | bytes 11796484
  125.9 2.4 %copy-start.1 = (bf16[4,2,8,16,1920]{4,3,2,1,0:T(8,128)(2,1)S(1)}, bf16[4,2,8,16,1920]{4,3,2,1,0:T(8,128)(2,1)}, u32[]{:S(2)}) copy-start(bf16[4,2,8,16,1920]{4,3,2,1,0:T(8,128)(2,1)} %get-tuple-element.12) | copy-start | bytes 11796484
  125.9 2.7 %copy-start.5 = (bf16[512,1920]{1,0:T(8,128)(2,1)S(1)}, bf16[512,1920]{1,0:T(8,128)(2,1)}, u32[]{:S(2)}) copy-start(bf16[512,1920]{1,0:T(8,128)(2,1)} %up_hbm.1) | copy-start | bytes 5898244
  148.3 1.2 copy-start
  149.5 6.6 %copy-start.2 = (bf16[4,2,8,16,1920]{4,3,2,1,0:T(8,128)(2,1)S(1)}, bf16[4,2,8,16,1920]{4,3,2,1,0:T(8,128)(2,1)}, u32[]{:S(2)}) copy-start(bf16[4,2,8,16,1920]{4,3,2,1,0:T(8,128)(2,1)} %get-tuple-element.12) | copy-start | bytes 11796484
  156.1 4.3 %copy-start.7 = (bf16[4,2,8,16,1920]{4,3,2,1,0:T(8,128)(2,1)S(1)}, bf16[4,2,8,16,1920]{4,3,2,1,0:T(8,128)(2,1)}, u32[]{:S(2)}) copy-start(bf16[4,2,8,16,1920]{4,3,2,1,0:T(8,128)(2,1)} %get-tuple-element.10) | copy-start | bytes 11796484
  156.1 4.3 %copy-start.8 = (bf16[4,2,128,512]{3,2,1,0:T(8,128)(2,1)S(1)}, bf16[4,2,128,512]{3,2,1,0:T(8,128)(2,1)}, u32[]{:S(2)}) copy-start(bf16[4,2,128,512]{3,2,1,0:T(8,128)(2,1)} %get-tuple-element.14) | copy-start | bytes 3145732
Sparse Core Ops, SparseCore 0:
  148.5 84.9 reduce-scatter.1

commit v2 on v1

--- a/solution.py
+++ b/solution.py
@@ -10,7 +10,7 @@
 WIDTH = 512
 HID = 1920
 ALL = 3 * HID
-CY = 3200
+CY = 3456
 CZ = ALL - CY
 HZ = CZ // 2
 UNIT = 640
@@ -18,14 +18,18 @@
 F32 = jnp.float32
 MESH = pl.DeviceIdType.MESH
 
-SEQ_NAMES = ["zh", "xo+", "xo-", "xp+", "xp-", "xf+", "xf-"]
+SEQ_NAMES = [
+    "zha", "zhg", "xoa+", "xoa-", "xog+", "xog-", "xpa+", "xpa-", "xpg+", "xpg-", "xf+", "xf-",
+    "sz", "dx+", "dx-", "dx2", "dz", "dzx+", "dzx-", "dzx2",
+]
 W_NAMES = ["wg", "wu", "wd"]
 CHUNK_NAMES = [
-    "q",
+    "qa", "qg",
     "y1+", "y1-", "yo+", "yo-", "ya+", "ya-", "yz",
     "z1", "r1+", "r1-", "ro+", "ro-", "ra+", "ra-",
     "az", "ay+", "ay-", "by+", "by-", "bz0", "ap+", "ap-", "bf+", "bf-",
     "bz1", "bz2", "af+", "af-", "bz3", "core",
+    "m+", "m-", "m2",
 ]
 SEM = {}
 for _n in SEQ_NAMES + W_NAMES:
@@ -45,11 +49,38 @@
     return value.astype(F32)
 
 
+def routing(lengths, destination, advantage, mask):
+    diagonal = lax.broadcasted_iota(jnp.int32, (16, 16), 0) == lax.broadcasted_iota(jnp.int32, (16, 16), 1)
+
+    def column(row):
+        return jnp.sum(jnp.where(diagonal, row, jnp.zeros_like(row)), axis=1, keepdims=True)
+
+    resp = lax.broadcasted_iota(jnp.int32, (16, 256), 0)
+    row = lax.broadcasted_iota(jnp.int32, (16, 256), 1)
+    of_row = row // BIN
+    mine = of_row == resp
+
+    def spread(col):
+        return jnp.sum(jnp.where(mine, col, jnp.zeros_like(col)), axis=0, keepdims=True)
+
+    len_col, dest_col = column(lengths), column(destination)
+    len_row, dest_row = spread(len_col), spread(dest_col)
+    before = (dest_col == dest_row) & (resp < of_row)
+    offset = jnp.sum(jnp.where(before, len_col, 0), axis=0, keepdims=True)
+    within = lax.rem(row[:1], BIN)
+    slot = jnp.where(within < len_row, dest_row * BIN + offset + within, -1)
+    hot = lax.broadcasted_iota(jnp.int32, (128, 256), 0) == slot
+    weight = spread(column(advantage)) * mask.astype(F32)
+    weight = jnp.sum(jnp.where(hot, weight, 0.0), axis=1, keepdims=True)
+    return jnp.where(hot, 1.0, 0.0).astype(BF), weight
+
+
 def mega(
-    acts_ref, grads_ref, hot_ref, weight_ref, gate_hbm, up_hbm, down_hbm,
-    hid_out, gg_out, gu_out, acts_out, grads_out,
+    acts_ref, grads_ref, lengths_ref, dest_ref, mask_ref, adv_ref, gate_hbm, up_hbm, down_hbm,
+    block_out, input_out, gate_out, up_out, down_out,
     wg, wu, wd, pg, pu, pd, G, Q, PP, H,
     y1, yown, yacc, ysend, yz, z1, r1, rown, racc, F,
+    OB, OL, rm, rp, r2, sz, rz, dr, tg, tu, td,
     ssem, rsem, lsem,
 ):
     s = lax.axis_index("seq")
@@ -64,6 +95,7 @@
 
     XP, XM = dev(x_=lax.rem(x + 1, 4)), dev(x_=lax.rem(x + 3, 4))
     YP, YM = dev(y_=yp), dev(y_=ym)
+    xp, xm, x2 = lax.rem(x + 1, 4), lax.rem(x + 3, 4), lax.rem(x + 2, 4)
     ZL, ZH, CO = dev(zl_=oz), dev(zh_=oh), dev(c_=oc)
 
     copies = {}
@@ -90,31 +122,37 @@
 
     loads = [local_copy(gate_hbm, wg), local_copy(up_hbm, wu), local_copy(down_hbm, wd)]
     barrier = pltpu.get_barrier_semaphore()
-    for peer in (XP, XM, YP, YM, ZL, ZH, CO):
+    peers = [XP, XM, YP, YM, ZL, ZH, CO, dev(x_=x2)]
+    peers += [dev(zh_=oh, x_=x_) for x_ in (xp, xm, x2)]
+    for peer in peers:
         pl.semaphore_signal(barrier, inc=1, device_id=peer, device_id_type=MESH)
 
-    hot = hot_ref[...]
+    hot, weight = routing(lengths_ref[...], dest_ref[...], adv_ref[...], mask_ref[...])
     G[0, 0, zh] = jnp.dot(hot, acts_ref[...], preferred_element_type=F32).astype(BF)
-    scaled = (up32(grads_ref[...]) * weight_ref[...]).astype(BF)
-    G[1, 0, zh] = jnp.dot(hot, scaled, preferred_element_type=F32).astype(BF)
-
-    pl.semaphore_wait(barrier, 7)
-
-    send("zh", 0, G.at[:, 0, zh], G.at[:, 0, zh], ZH)
-    send("xo+", 0, G.at[:, 0, zh], G.at[:, 1, zh], XP)
-    send("xo-", 0, G.at[:, 0, zh], G.at[:, 2, zh], XM)
+    pl.semaphore_wait(barrier, len(peers))
+    for arr, n in ((0, "a"), (1, "g")):
+        if arr == 1:
+            packed = jnp.dot(hot, grads_ref[...], preferred_element_type=F32)
+            G[1, 0, zh] = (packed * weight).astype(BF)
+        send("zh" + n, 0, G.at[arr, 0, zh], G.at[arr, 0, zh], ZH)
+        send("xo" + n + "+", 0, G.at[arr, 0, zh], G.at[arr, 1, zh], XP)
+        send("xo" + n + "-", 0, G.at[arr, 0, zh], G.at[arr, 2, zh], XM)
     for cp, name, src, dst in zip(loads, W_NAMES, (wg, wu, wd), (pg, pu, pd)):
         cp.wait()
         send(name, 0, src, dst, CO)
-    recv("zh", 0)
-    send("q", 0, G.at[:, 0, oc], Q.at[:, 0], CO)
-    send("xp+", 0, G.at[:, 0, oh], G.at[:, 1, oh], XP)
-    send("xp-", 0, G.at[:, 0, oh], G.at[:, 2, oh], XM)
+    for arr, n in ((0, "a"), (1, "g")):
+        recv("zh" + n, 0)
+        send("q" + n, 0, G.at[arr, 0, oc], Q.at[arr, 0], CO)
+        send("xp" + n + "+", 0, G.at[arr, 0, oh], G.at[arr, 1, oh], XP)
+        send("xp" + n + "-", 0, G.at[arr, 0, oh], G.at[arr, 2, oh], XM)
 
     def forward(k):
-        recv("q", k)
+        recv("qa", k)
         a_own, a_par = G[0, k, c], Q[0, k]
-        for own, par, first in ((wg, pg, 0), (wu, pu, HID)):
+        for own, par, first, name in ((wg, pg, 0, "wg"), (wu, pu, HID, "wu")):
+            if k == 0:
+                recv(name, 0)
+
             def unit(u, carry, own=own, par=par, first=first):
                 cols = pl.ds(pl.multiple_of(u * UNIT, 128), UNIT)
                 to = pl.ds(pl.multiple_of(u * UNIT + first, 128), UNIT)
@@ -127,6 +165,9 @@
         send("y1-", k, PP.at[k, 4 + y2, :, YCOL], y1.at[k, 1], YM)
         send("yo+", k, PP.at[k, 4 + yp, :, YCOL], yown.at[k, 1], YP)
         send("yo-", k, PP.at[k, ym, :, YCOL], yown.at[k, 0], YM)
+        recv("qg", k)
+        if k == 0:
+            recv("wd", 0)
         g_own, g_par = G[1, k, c], Q[1, k]
 
         def unit_back(u, carry):
@@ -235,28 +276,110 @@
 
     def last(k):
         recv("core", k)
-        for first, out in ((0, hid_out), (HID, gg_out), (2 * HID, gu_out)):
-            local_copy(H.at[k, :, :, :, pl.ds(first, HID)], out.at[k])
+        nt = (((1,), (1,)), ((), ()))
+        shape = (2, 2, 4, BIN, WIDTH)
+        h = H[k, :, :, :, :HID].reshape(256, HID)
+        part = jnp.dot(h, wd[...], preferred_element_type=F32).reshape(shape)
+        OB[k, :, :, :, :, :WIDTH] = part
+        if k == NC - 1:
+            OL[:, :, :, :, :WIDTH] = part.astype(BF)
+        h = H[k, :, :, :, HID:2 * HID].reshape(256, HID)
+        part = lax.dot_general(h, wg[...], nt, preferred_element_type=F32)
+        h = H[k, :, :, :, 2 * HID:].reshape(256, HID)
+        part += lax.dot_general(h, wu[...], nt, preferred_element_type=F32)
+        part = part.reshape(shape)
+        OB[k, :, :, :, :, WIDTH:] = part
+        if k < NC - 1:
+            send("m+", k, OB.at[k, :, :, xp], rm.at[k], XP)
+            send("m-", k, OB.at[k, :, :, xm], rp.at[k], XM)
+            send("m2", k, OB.at[k, :, :, x2], r2.at[k], dev(x_=x2))
+        else:
+            OL[:, :, :, :, WIDTH:] = part.astype(BF)
+            send("dzx2", 0, OL.at[:, oh, x2], dr.at[6], dev(zh_=oh, x_=x2))
+            send("dzx+", 0, OL.at[:, oh, xp], dr.at[4], dev(zh_=oh, x_=xp))
+            send("dzx-", 0, OL.at[:, oh, xm], dr.at[5], dev(zh_=oh, x_=xm))
+            send("dz", 0, OL.at[:, oh, x], dr.at[3], ZH)
+            send("dx2", 0, OL.at[:, zh, x2], dr.at[2], dev(x_=x2))
+            send("dx+", 0, OL.at[:, zh, xp], dr.at[0], XP)
+            send("dx-", 0, OL.at[:, zh, xm], dr.at[1], XM)
+
+    PLACES = ((0, 2, 1, 3), (2, 3, 0, 1), (3, 1, 2, 0), (1, 0, 3, 2))
+
+    def earlier_sum(r, half):
+        total = None
+        for k, ref in zip(PLACES[r], (None, rm, rp, r2)):
+            if k < NC - 1:
+                part = OB[k, :, half, x] if ref is None else ref[k, :, half]
+                total = part if total is None else total + part
+        return total
+
+    def seq_exchange():
+        for k in range(NC - 1):
+            for name in ("m+", "m-", "m2"):
+                recv(name, k)
+        for r in range(4):
+            sz[r] = earlier_sum(r, oh).astype(BF)
+        send("sz", 0, sz, rz, ZH)
+
+    def seq_finish():
+        for name in ("dx+", "dx-", "dx2", "dz", "dzx+", "dzx-", "dzx2", "sz"):
+            recv(name, 0)
+        late = {0: (2, 6), 1: (0, 4), 2: (3,), 3: (1, 5)}
+        for r in range(4):
+            total = earlier_sum(r, zh) + up32(rz[r])
+            for j in late[r]:
+                total += up32(dr[j])
+            if r == 2:
+                total += OB[NC - 1, :, zh, x]
+            total = total.astype(BF)
+            source = lax.rem(x + r, 4)
+            block_out[:, source] = total[:, :, :WIDTH]
+            input_out[:, source] = total[:, :, WIDTH:]
+
+    def pair_grads():
+        tn = (((0,), (0,)), ((), ()))
+        acts = G[0].reshape(1024, WIDTH)
+        for first, to in ((HID, tg), (2 * HID, tu)):
+            def unit(u, carry, first=first, to=to):
+                cols = pl.ds(pl.multiple_of(u * UNIT + first, 128), UNIT)
+                h = H[:, :, :, :, cols].reshape(1024, UNIT)
+                part = lax.dot_general(acts, h, tn, preferred_element_type=F32)
+                to[:, pl.ds(pl.multiple_of(u * UNIT, 128), UNIT)] = (part * (1.0 / 32.0)).astype(BF)
+                return carry
+            lax.fori_loop(0, 3, unit, 0)
+        local_copy(tg, gate_out)
+        local_copy(tu, up_out)
+
+    def down_grads():
+        tn = (((0,), (0,)), ((), ()))
+        grads = G[1].reshape(1024, WIDTH)
+
+        def unit(u, carry):
+            cols = pl.ds(pl.multiple_of(u * UNIT, 128), UNIT)
+            h = H[:, :, :, :, cols].reshape(1024, UNIT)
+            part = lax.dot_general(h, grads, tn, preferred_element_type=F32)
+            td[cols, :] = (part * (1.0 / 32.0)).astype(BF)
+            return carry
+        lax.fori_loop(0, 3, unit, 0)
+        local_copy(td, down_out)
 
     def seq_one():
-        for name in ("xo+", "xp+", "xo-", "xp-"):
+        for name in ("xoa+", "xpa+", "xoa-", "xpa-", "xog+", "xpg+", "xog-", "xpg-"):
             recv(name, 0)
         send("xf+", 0, G.at[:, 1, 0], G.at[:, 3, 0], XP)
         send("xf-", 0, G.at[:, 2, 1], G.at[:, 3, 1], XM)
-        send("q", 1, G.at[:, 1, oc], Q.at[:, 1], CO)
-        send("q", 2, G.at[:, 2, oc], Q.at[:, 2], CO)
+        for k in (1, 2):
+            send("qa", k, G.at[0, k, oc], Q.at[0, k], CO)
+            send("qg", k, G.at[1, k, oc], Q.at[1, k], CO)
 
     def seq_two():
         recv("xf+", 0)
         recv("xf-", 0)
-        send("q", 3, G.at[:, 3, oc], Q.at[:, 3], CO)
-        local_copy(G.at[0], acts_out)
-        local_copy(G.at[1], grads_out)
-
-    for name in W_NAMES:
-        recv(name, 0)
-    stages = [forward, reduce_one, reduce_two, finish, gather_one, gather_two, gather_three, last]
-    for slot in range(NC + len(stages) - 1):
+        send("qa", 3, G.at[0, 3, oc], Q.at[0, 3], CO)
+        send("qg", 3, G.at[1, 3, oc], Q.at[1, 3], CO)
+
+    stages = [forward, reduce_one, reduce_two, finish, gather_one, gather_two, gather_three]
+    for slot in range(NC + len(stages)):
         if slot < NC:
             forward(slot)
         if slot == 0:
@@ -267,22 +390,30 @@
             stage = slot - k
             if 1 <= stage < len(stages):
                 stages[stage](k)
+        if 0 <= slot - len(stages) < NC:
+            last(slot - len(stages))
+    pair_grads()
+    seq_exchange()
+    down_grads()
+    seq_finish()
     for cp in copies.values():
         cp.wait_send()
     for cp in local[len(loads):]:
         cp.wait()
 
 
-def run_mega(acts, grads, hot, weight, gate, up, down):
+def run_mega(acts, grads, lengths, dest, mask, adv, gate, up, down):
     vm = pltpu.VMEM
     shape = jax.ShapeDtypeStruct
-    rows = shape((NC, 2, 8, BIN, HID), BF)
-    packed = shape((NC, 2, 128, WIDTH), BF)
+    rows = shape((2, 4, BIN, WIDTH), BF)
+    wide, tall = shape((WIDTH, HID), BF), shape((HID, WIDTH), BF)
+    hbm = pl.BlockSpec(memory_space=pl.ANY)
+    whole = pl.BlockSpec(memory_space=vm)
     return pl.pallas_call(
         mega,
-        out_shape=(rows, rows, rows, packed, packed),
-        in_specs=[pl.BlockSpec(memory_space=vm)] * 4 + [pl.BlockSpec(memory_space=pl.ANY)] * 3,
-        out_specs=tuple([pl.BlockSpec(memory_space=pl.ANY)] * 5),
+        out_shape=(rows, rows, wide, wide, tall),
+        in_specs=[whole] * 6 + [hbm] * 3,
+        out_specs=(whole, whole, hbm, hbm, hbm),
         scratch_shapes=[
             vm((WIDTH, HID), BF), vm((WIDTH, HID), BF), vm((HID, WIDTH), BF),
             vm((WIDTH, HID), BF), vm((WIDTH, HID), BF), vm((HID, WIDTH), BF),
@@ -295,55 +426,37 @@
             vm((NC, 4, BIN, CZ), BF),
             vm((NC, 2, BIN, HZ), BF), vm((NC, 2, BIN, HZ), BF), vm((NC, 2, BIN, HZ), BF),
             vm((BIN, ALL), F32),
+            vm((NC, 2, 2, 4, BIN, 2 * WIDTH), F32),
+            vm((2, 2, 4, BIN, 2 * WIDTH), BF),
+            vm((NC - 1, 2, 2, BIN, 2 * WIDTH), F32),
+            vm((NC - 1, 2, 2, BIN, 2 * WIDTH), F32),
+            vm((NC - 1, 2, 2, BIN, 2 * WIDTH), F32),
+            vm((4, 2, BIN, 2 * WIDTH), BF), vm((4, 2, BIN, 2 * WIDTH), BF),
+            vm((7, 2, BIN, 2 * WIDTH), BF),
+            vm((WIDTH, HID), BF), vm((WIDTH, HID), BF), vm((HID, WIDTH), BF),
             pltpu.SemaphoreType.DMA((N_SEM,)),
             pltpu.SemaphoreType.DMA((N_SEM,)),
-            pltpu.SemaphoreType.DMA((32,)),
+            pltpu.SemaphoreType.DMA((8,)),
         ],
         compiler_params=pltpu.CompilerParams(
-            collective_id=0, has_side_effects=True, vmem_limit_bytes=60 * 2**20
+            collective_id=0, has_side_effects=True, vmem_limit_bytes=62 * 2**20
         ),
         name="mega",
-    )(acts, grads, hot, weight, gate, up, down)
+    )(acts, grads, lengths, dest, mask, adv, gate, up, down)
 
 
 def per_device(
     rollout_acts, rollout_grads, lengths, destination, valid_mask, advantage,
     gate_weight, up_weight, down_weight,
 ):
-    x = lax.rem(lax.axis_index("seq"), 4)
-    own_lengths = lengths[0]
-    own_dest = destination[0]
-    order = jnp.arange(own_dest.shape[0])
-    same = own_dest[:, None] == own_dest[None, :]
-    earlier = order[None, :] < order[:, None]
-    offsets = jnp.sum(jnp.where(same & earlier, own_lengths[None, :], 0), axis=1)
-    within = jnp.arange(BIN)
-    target = own_dest[:, None] * BIN + offsets[:, None] + within[None, :]
-    live = within[None, :] < own_lengths[:, None]
-    target = jnp.where(live, target, -1).reshape(-1)
-    hot = (jnp.arange(8 * BIN)[:, None] == target[None, :]).astype(BF)
-    row_weight = jnp.repeat(advantage[0], BIN) * valid_mask.astype(F32)
-    hidden, gg, gu, acts, grads = run_mega(
-        rollout_acts, rollout_grads, hot, row_weight[:, None], gate_weight, up_weight, down_weight
+    block, inner, gate_grad, up_grad, down_grad = run_mega(
+        rollout_acts, rollout_grads, lengths, destination, valid_mask[None, :], advantage,
+        gate_weight, up_weight, down_weight,
     )
-    total = 1024
-    hidden, gg, gu = (v.reshape(total, HID) for v in (hidden, gg, gu))
-    acts, grads = acts.reshape(total, WIDTH), grads.reshape(total, WIDTH)
-    block = jnp.dot(hidden, down_weight, preferred_element_type=F32)
-    nt = (((1,), (1,)), ((), ()))
-    inner = lax.dot_general(gg, gate_weight, nt, preferred_element_type=F32)
-    inner += lax.dot_general(gu, up_weight, nt, preferred_element_type=F32)
-    both = jnp.concatenate([block, inner], axis=1).reshape(NC, 2, 8, BIN, 2 * WIDTH)
-    chunk_of = jnp.array([0, 2, 3, 1])[lax.rem(jnp.arange(4) - x + 4, 4)]
-    both = both[chunk_of]
-    both = both.transpose(2, 1, 0, 3, 4).reshape(total, 2 * WIDTH)
-    both = lax.psum_scatter(both, "seq", scatter_dimension=0, tiled=True).astype(BF)
-    scale = 1.0 / jnp.sqrt(jnp.float32(total))
-    tn = (((0,), (0,)), ((), ()))
-    gate_grad = lax.dot_general(acts, gg, tn, preferred_element_type=F32) * scale
-    up_grad = lax.dot_general(acts, gu, tn, preferred_element_type=F32) * scale
-    down_grad = lax.dot_general(hidden, grads, tn, preferred_element_type=F32) * scale
-    return both[:, :WIDTH], both[:, WIDTH:], gate_grad, up_grad, down_grad
+    return (
+        block.reshape(128, WIDTH), inner.reshape(128, WIDTH),
+        gate_grad.astype(F32), up_grad.astype(F32), down_grad.astype(F32),
+    )
 
 
 def solution(mesh):

time: 243 us -> 157 us (0.65)
  waiting for transfers between devices: 68.9 us -> 0 us
  Pallas kernels: 107 us -> 146 us
  matrix products: 24.5 us -> 0 us
  local copies, waits for them, and re-layouts: 20.3 us -> 1.43 us
  between operations: 14.2 us -> 0.66 us
    reduce_scatter x1 -> x0, waiting for transfers between devices: 68.9 us -> none  [per_device(): lax.psum_scatter(both, 'seq', scatter_dimension=0, tiled=True).astype(BF)]
    pallas_call x1, Pallas kernels: 107 us -> 146 us  [run_mega(): pl.pallas_call(mega, out_shape=(rows, rows, wide, wide, tall), in_specs=[...]
    dot_general x6 -> x0, matrix products: 24.5 us -> none  [the longest x1 6.55 us: per_device(): lax.dot_general(acts, gg, tn, preferred_element_type=F32) * scale]
    convert_element_type x2 -> x3, other arithmetic: 1.72 us -> 8.55 us  [the longest x1 3.88 us: per_device(): gate_grad.astype(F32)]
    gather x2 -> x0, local copies, waits for them, and re-layouts: 6.27 us -> none  [the longest x1 4.98 us: per_device(): both = both[chunk_of]]
    concatenate x1 -> x0, local copies, waits for them, and re-layouts: 5.35 us -> none  [per_device(): jnp.concatenate([block, inner], axis=1).reshape(NC, 2, 8, BIN, 2 * WIDTH)]
    transpose x1 -> x0, local copies, waits for them, and re-layouts: 4.71 us -> none  [per_device(): both = both.transpose(2, 1, 0, 3, 4).reshape(total, 2 * WIDTH)]
  transfers between devices with their start and end apart: 1 -> 0, of which waited for: 1 -> 0; matrix products, arithmetic and copies ran while one was open for 6% -> 0% of each run, Pallas kernels for 0% -> 0%
where the time goes in v2:
time: 157 us
  Pallas kernels  146 us (93%)
  other arithmetic  8.55 us (5%)
    pallas_call x1, Pallas kernels, run_mega(): pl.pallas_call(mega, out_shape=(rows, rows, wide, wide, tall), in_specs=[...  146 us
    convert_element_type x1, other arithmetic, per_device(): gate_grad.astype(F32)  3.88 us

profile of v2, /device:TPU:0, one launch (start us, length us, event | category | flops | bytes accessed | tf_op | source)
XLA Modules:
  0.0 157.0 jit_solution(12826178731473415981)
XLA Ops:
  0.6 146.4 %mega.1 = (bf16[2,4,16,512]{3,2,1,0:T(8,128)(2,1)}, bf16[2,4,16,512]{3,2,1,0:T(8,128)(2,1)}, bf16[512,1920]{1,0:T(8,128)(2,1)}, bf16[512,1920]{1,0:T(8,128)(2,1)}, bf16[1920,512]{1,0:T(8,128)(2,1)}) custom-call(bf16[256,512]{1,0:T(8,128)(2,1)} %acts_ref.1, bf16[256,512]{1,0:T(8,128)(2,1)} %grads_ref.1, s32[1,16]{1,0:T(1,128)} %lengths_ref.1, ...), custom_call_target="tpu_custom_call" | custom-call | tf_op jit(solution)/shard_map/mega/pallas_call | solution.py:412
  147.0 0.0 copy-start.1
  147.0 3.9 %convert_element_type.9 = f32[512,1920]{1,0:T(8,128)} convert(bf16[512,1920]{1,0:T(8,128)(2,1)} %get-tuple-element.12) | non-fusion elementwise | flops 983040 | bytes 5898240 | tf_op jit(solution)/shard_map/convert_element_type | solution.py:458
  150.9 0.0 copy-done.1
  150.9 0.0 copy-start
  150.9 2.2 %convert_element_type.10 = f32[512,1920]{1,0:T(8,128)} convert(bf16[512,1920]{1,0:T(8,128)(2,1)S(1)} %copy-done.1) | non-fusion elementwise | flops 983040 | bytes 5898240 | tf_op jit(solution)/shard_map/convert_element_type | solution.py:458
  153.1 0.1 copy-done
  153.2 0.0 copy-start.3
  153.2 0.0 copy-start.2
  153.2 2.5 %convert_element_type.11 = f32[1920,512]{1,0:T(8,128)} convert(bf16[1920,512]{1,0:T(8,128)(2,1)S(1)} %copy-done) | non-fusion elementwise | flops 983040 | bytes 5898240 | tf_op jit(solution)/shard_map/convert_element_type | solution.py:458
  155.7 0.0 copy-done.3
  155.7 0.7 copy.16
  156.3 0.0 copy-done.2
  156.3 0.7 copy.17
Async XLA Ops:
  147.0 3.9 %copy-start.1 = (bf16[512,1920]{1,0:T(8,128)(2,1)S(1)}, bf16[512,1920]{1,0:T(8,128)(2,1)}, u32[]{:S(2)}) copy-start(bf16[512,1920]{1,0:T(8,128)(2,1)} %get-tuple-element.13) | copy-start | bytes 5898244
  150.9 2.3 %copy-start = (bf16[1920,512]{1,0:T(8,128)(2,1)S(1)}, bf16[1920,512]{1,0:T(8,128)(2,1)}, u32[]{:S(2)}) copy-start(bf16[1920,512]{1,0:T(8,128)(2,1)} %get-tuple-element.14) | copy-start | bytes 5898244
  153.2 2.5 %copy-start.3 = (bf16[2,4,16,512]{3,2,1,0:T(8,128)(2,1)S(1)}, bf16[2,4,16,512]{3,2,1,0:T(8,128)(2,1)}, u32[]{:S(2)}) copy-start(bf16[2,4,16,512]{3,2,1,0:T(8,128)(2,1)} %get-tuple-element.10) | copy-start | bytes 393220
  153.2 3.1 %copy-start.2 = (bf16[2,4,16,512]{3,2,1,0:T(8,128)(2,1)S(1)}, bf16[2,4,16,512]{3,2,1,0:T(8,128)(2,1)}, u32[]{:S(2)}) copy-start(bf16[2,4,16,512]{3,2,1,0:T(8,128)(2,1)} %get-tuple-element.11) | copy-start | bytes 393220

commit v3 on v2

v3 whole, which is shorter than its diff:
```python
import jax
import jax.numpy as jnp
from jax import lax
from jax.experimental import pallas as pl
from jax.experimental.pallas import tpu as pltpu
from jax.sharding import PartitionSpec as P

BIN = 16
NS = 4
WIDTH = 512
HID = 1920
PARTS = (1920,)
YCOLS = (3456,)
NP = len(PARTS)
NK = NS * NP
BASES = tuple(sum(PARTS[:j]) for j in range(NP))
ALL = 3 * HID
MAXY = max(YCOLS)
MAXZ = max(3 * h - w for h, w in zip(PARTS, YCOLS))
BF = jnp.bfloat16
F32 = jnp.float32
MESH = pl.DeviceIdType.MESH
NT = (((1,), (1,)), ((), ()))
TN = (((0,), (0,)), ((), ()))

ORDER = (
    ("pro", 0), ("pro2", 0), ("wl", 0), ("zha", 0), ("zhg", 0), ("fa", 0), ("fb", 0), ("sx", 0), ("ya+", 0),
    ("ya-", 0), ("fa", 1), ("fb", 1), ("yz", 0), ("sy", 0), ("zr", 0), ("fa", 2), ("ya+", 1), ("ya-", 1),
    ("fb", 2), ("ra+", 0), ("ra-", 0), ("zr", 1), ("ya+", 2), ("ya-", 2), ("yz", 1), ("fin", 0), ("ra+", 1),
    ("ra-", 1), ("zr", 2), ("yz", 2), ("ap", 0), ("af+", 0), ("bp", 0), ("bm", 0), ("ca", 0), ("fin", 1),
    ("ra+", 2), ("ra-", 2), ("af-", 0), ("ap", 1), ("b3", 0), ("fa", 3), ("bm", 1), ("af+", 1), ("fb", 3),
    ("bp", 1), ("ca", 1), ("fin", 2), ("cc", 0), ("af-", 1), ("last", 0), ("ya+", 3), ("ya-", 3), ("zr", 3),
    ("b3", 1), ("ap", 2), ("bm", 2), ("af+", 2), ("bp", 2), ("cc", 1), ("ca", 2), ("yz", 3), ("ra+", 3),
    ("ra-", 3), ("last", 1), ("af-", 2), ("b3", 2), ("fin", 3), ("cc", 2), ("af+", 3), ("ap", 3),
    ("last", 2), ("bp", 3), ("bm", 3), ("ca", 3), ("af-", 3), ("b3", 3), ("sz", 0), ("cc", 3), ("last", 3),
    ("wgrad", 0), ("end", 0),
)

SEQ_NAMES = (
    "zha", "zhg", "xoa+", "xoa-", "xog+", "xog-", "xpa+", "xpa-", "xpg+", "xpg-", "xf+", "xf-",
    "sz", "dx+", "dx-", "dx2", "dz", "dzx+", "dzx-", "dzx2",
)
PIECE_NAMES = (
    "y1+", "y1-", "yo+", "yo-", "ya+", "ya-", "yz",
    "z1", "r1+", "r1-", "ro+", "ro-", "ra+", "ra-",
    "az", "ay+", "ay-", "by+", "by-", "bz0", "ap+", "ap-", "bf+", "bf-",
    "bz1", "bz2", "af+", "af-", "bz3", "ca0", "ca1", "ca2", "cc0", "cc1",
)
SEM = {}
for _n in SEQ_NAMES:
    SEM[(_n, 0)] = len(SEM)
for _k in range(NP):
    for _n in ("wg", "wu", "wd"):
        SEM[(_n, _k)] = len(SEM)
for _k in range(NS):
    for _n in ("qa", "qg", "m+", "m-", "m2"):
        SEM[(_n, _k)] = len(SEM)
for _k in range(NK):
    for _n in PIECE_NAMES:
        SEM[(_n, _k)] = len(SEM)
N_SEM = len(SEM)


def up32(value):
    return value.astype(F32)


def routing(lengths, destination, advantage, mask):
    diagonal = lax.broadcasted_iota(jnp.int32, (16, 16), 0) == lax.broadcasted_iota(jnp.int32, (16, 16), 1)

    def column(row):
        return jnp.sum(jnp.where(diagonal, row, jnp.zeros_like(row)), axis=1, keepdims=True)

    resp = lax.broadcasted_iota(jnp.int32, (16, 256), 0)
    row = lax.broadcasted_iota(jnp.int32, (16, 256), 1)
    of_row = row // BIN
    mine = of_row == resp

    def spread(col):
        return jnp.sum(jnp.where(mine, col, jnp.zeros_like(col)), axis=0, keepdims=True)

    len_col, dest_col = column(lengths), column(destination)
    len_row, dest_row = spread(len_col), spread(dest_col)
    before = (dest_col == dest_row) & (resp < of_row)
    offset = jnp.sum(jnp.where(before, len_col, 0), axis=0, keepdims=True)
    within = lax.rem(row[:1], BIN)
    slot = jnp.where(within < len_row, dest_row * BIN + offset + within, -1)
    hot = lax.broadcasted_iota(jnp.int32, (128, 256), 0) == slot
    weight = spread(column(advantage)) * mask.astype(F32)
    weight = jnp.sum(jnp.where(hot, weight, 0.0), axis=1, keepdims=True)
    return jnp.where(hot, 1.0, 0.0).astype(BF), weight


def mega(
    acts_ref, grads_ref, lengths_ref, dest_ref, mask_ref, adv_ref, gate_hbm, up_hbm, down_hbm,
    block_out, input_out, gate_out, up_out, down_out,
    wg, wu, wd, pg, pu, pd, G, Q, RY, RZ, FY, FZ, H,
    y1, yown, yacc, ysend, yz, z1, r1, rown, racc, F,
    OB, OL, rm, rp, r2, sz, rz, dr, tg, tu, td,
    ssem, rsem, lsem,
):
    s = lax.axis_index("seq")
    t = lax.axis_index("tp")
    zh, x = s // 4, lax.rem(s, 4)
    zl, y, c = t // 8, lax.rem(t // 2, 4), lax.rem(t, 2)
    oz, oc, oh = 1 - zl, 1 - c, 1 - zh
    yp, ym, y2 = lax.rem(y + 1, 4), lax.rem(y + 3, 4), lax.rem(y + 2, 4)
    xp, xm, x2 = lax.rem(x + 1, 4), lax.rem(x + 3, 4), lax.rem(x + 2, 4)

    def dev(zh_=zh, x_=x, zl_=zl, y_=y, c_=c):
        return (zh_ * 4 + x_, zl_ * 8 + y_ * 2 + c_)

    XP, XM, X2 = dev(x_=xp), dev(x_=xm), dev(x_=x2)
    YP, YM = dev(y_=yp), dev(y_=ym)
    ZL, ZH, CO = dev(zl_=oz), dev(zh_=oh), dev(c_=oc)

    copies = {}

    def send(name, k, src, dst, to):
        i = SEM[(name, k)]
        cp = pltpu.make_async_remote_copy(
            src_ref=src, dst_ref=dst, send_sem=ssem.at[i], recv_sem=rsem.at[i],
            device_id=to, device_id_type=MESH,
        )
        cp.start()
        copies[(name, k)] = cp

    def recv(k, *names):
        for name in names:
            copies[(name, k)].wait_recv()

    local = []

    def local_copy(src, dst):
        cp = pltpu.make_async_copy(src, dst, lsem.at[len(local)])
        cp.start()
        local.append(cp)
        return cp

    def src_of(k):
        return k // NP

    def hid_of(k):
        return pl.ds(BASES[k % NP], PARTS[k % NP])

    def sizes(k):
        h, w = PARTS[k % NP], YCOLS[k % NP]
        return h, w, 3 * h - w, (3 * h - w) // 2

    def all_cols(k):
        return pl.ds(3 * BASES[k % NP], 3 * PARTS[k % NP])

    def y_cols(k):
        return pl.ds(3 * BASES[k % NP], YCOLS[k % NP])

    def z_cols(k):
        return pl.ds(3 * BASES[k % NP] + YCOLS[k % NP], sizes(k)[2])

    def z_half(k, half):
        return pl.ds(3 * BASES[k % NP] + YCOLS[k % NP] + half * sizes(k)[3], sizes(k)[3])

    loads = [local_copy(gate_hbm, wg), local_copy(up_hbm, wu), local_copy(down_hbm, wd)]
    barrier = pltpu.get_barrier_semaphore()
    peers = [XP, XM, YP, YM, ZL, ZH, CO, X2]
    peers += [dev(zh_=oh, x_=x_) for x_ in (xp, xm, x2)]
    for peer in peers:
        pl.semaphore_signal(barrier, inc=1, device_id=peer, device_id_type=MESH)
    hot, weight = routing(lengths_ref[...], dest_ref[...], adv_ref[...], mask_ref[...])

    def spread_own(arr, n):
        send("zh" + n, 0, G.at[arr, 0, zh], G.at[arr, 0, zh], ZH)
        send("xo" + n + "+", 0, G.at[arr, 0, zh], G.at[arr, 1, zh], XP)
        send("xo" + n + "-", 0, G.at[arr, 0, zh], G.at[arr, 2, zh], XM)

    def spread_peer(arr, n):
        recv(0, "zh" + n)
        send("q" + n, 0, G.at[arr, 0, oc], Q.at[arr, 0], CO)
        send("xp" + n + "+", 0, G.at[arr, 0, oh], G.at[arr, 1, oh], XP)
        send("xp" + n + "-", 0, G.at[arr, 0, oh], G.at[arr, 2, oh], XM)

    def pack_acts(k):
        G[0, 0, zh] = jnp.dot(hot, acts_ref[...], preferred_element_type=F32).astype(BF)
        pl.semaphore_wait(barrier, len(peers))
        spread_own(0, "a")

    def pack_grads(k):
        packed = jnp.dot(hot, grads_ref[...], preferred_element_type=F32)
        G[1, 0, zh] = (packed * weight).astype(BF)
        spread_own(1, "g")

    def swap_weights(k):
        for cp in loads:
            cp.wait()
        for j in range(NP):
            hid = hid_of(j)
            send("wg", j, wg.at[:, hid], pg.at[:, hid], CO)
            send("wu", j, wu.at[:, hid], pu.at[:, hid], CO)
            send("wd", j, wd.at[hid], pd.at[hid], CO)

    def peer_acts(k):
        spread_peer(0, "a")

    def peer_grads(k):
        spread_peer(1, "g")

    def pass_on(k):
        recv(0, "xoa+", "xpa+", "xoa-", "xpa-", "xog+", "xpg+", "xog-", "xpg-")
        send("xf+", 0, G.at[:, 1, 0], G.at[:, 3, 0], XP)
        send("xf-", 0, G.at[:, 2, 1], G.at[:, 3, 1], XM)
        for n in (1, 2):
            send("qa", n, G.at[0, n, oc], Q.at[0, n], CO)
            send("qg", n, G.at[1, n, oc], Q.at[1, n], CO)

    def far_rows(k):
        recv(0, "xf+", "xf-")
        send("qa", 3, G.at[0, 3, oc], Q.at[0, 3], CO)
        send("qg", 3, G.at[1, 3, oc], Q.at[1, 3], CO)

    Y_ORDER = ((0, y2), (1, y2), (1, yp), (0, ym), (0, yp), (1, ym), (0, y), (1, y))
    Z_ORDER = tuple((oz, n) for n in range(4)) + tuple((zl, n) for n in range(4))

    def rows_in(ref, index, order):
        return jnp.concatenate(
            [ref[index + (pl.ds(pl.multiple_of((a * 4 + b) * BIN, BIN), BIN),)] for a, b in order], axis=0
        )

    def keep(raw, full, k, first, part):
        width = part.shape[1]
        raw[k, :, :, first:first + width] = part[:64].astype(BF).reshape(4, BIN, width)
        full[k, :, :, first:first + width] = part[64:].reshape(4, BIN, width)

    def product(a, b, own, par):
        return jnp.dot(a, own, preferred_element_type=F32) + jnp.dot(b, par, preferred_element_type=F32)

    def forward_y(k):
        n, j = src_of(k), k % NP
        h, w, _, _ = sizes(k)
        base = BASES[j]
        recv(n, "qa") if j == 0 else None
        recv(j, "wg", "wu") if n == 0 else None
        a, b = rows_in(G, (0, n, c), Y_ORDER), rows_in(Q, (0, n), Y_ORDER)
        cols = slice(base, base + h)
        keep(RY, FY, k, 0, product(a, b, wg[:, cols], pg[:, cols]))
        cols = slice(base, base + w - h)
        keep(RY, FY, k, h, product(a, b, wu[:, cols], pu[:, cols]))
        send("y1+", k, RY.at[k, 0, :, pl.ds(0, w)], y1.at[k, 0, :, pl.ds(0, w)], YP)
        send("y1-", k, RY.at[k, 1, :, pl.ds(0, w)], y1.at[k, 1, :, pl.ds(0, w)], YM)
        send("yo+", k, RY.at[k, 2, :, pl.ds(0, w)], yown.at[k, 1, :, pl.ds(0, w)], YP)
        send("yo-", k, RY.at[k, 3, :, pl.ds(0, w)], yown.at[k, 0, :, pl.ds(0, w)], YM)

    def forward_z(k):
        n, j = src_of(k), k % NP
        h, w, v, _ = sizes(k)
        base = BASES[j]
        a, b = rows_in(G, (0, n, c), Z_ORDER), rows_in(Q, (0, n), Z_ORDER)
        cols = slice(base + w - h, base + h)
        keep(RZ, FZ, k, 0, product(a, b, wu[:, cols], pu[:, cols]))
        recv(n, "qg") if j == 0 else None
        recv(j, "wd") if n == 0 else None
        a, b = rows_in(G, (1, n, c), Z_ORDER), rows_in(Q, (1, n), Z_ORDER)
        part = lax.dot_general(a, wd[base:base + h, :], NT, preferred_element_type=F32)
        part += lax.dot_general(b, pd[base:base + h, :], NT, preferred_element_type=F32)
        keep(RZ, FZ, k, 2 * h - w, part)
        send("z1", k, RZ.at[k, :, :, pl.ds(0, v)], z1.at[k, :, :, pl.ds(0, v)], ZL)

    def pass_y(k, half, name, to):
        w = sizes(k)[1]
        recv(k, "y1" + name)
        y1[k, half, :, :w] = (up32(y1[k, half, :, :w]) + FY[k, half, :, :w]).astype(BF)
        send("ya" + name, k, y1.at[k, half, :, pl.ds(0, w)], yacc.at[k, half, :, pl.ds(0, w)], to)

    def pass_z(k):
        _, _, v, u = sizes(k)
        recv(k, "z1")
        for row in (y2, yp, ym):
            z1[k, row, :, :v] = (up32(z1[k, row, :, :v]) + FZ[k, row, :, :v]).astype(BF)
        low, high = pl.ds(0, u), pl.ds(u, u)
        send("r1+", k, z1.at[k, y2, :, low], r1.at[k, 0, :, low], YP)
        send("r1-", k, z1.at[k, y2, :, high], r1.at[k, 1, :, low], YM)
        send("ro+", k, z1.at[k, yp, :, high], rown.at[k, 1, :, low], YP)
        send("ro-", k, z1.at[k, ym, :, low], rown.at[k, 0, :, low], YM)

    def cross_z(k):
        w = sizes(k)[1]
        recv(k, "yo+", "yo-", "ya+", "ya-")
        total = FY[k, 2 + oz, :, :w] + up32(yacc[k, oz, :, :w]) + up32(yown[k, oz, :, :w])
        ysend[k, :, :w] = total.astype(BF)
        send("yz", k, ysend.at[k, :, pl.ds(0, w)], yz.at[k, :, pl.ds(0, w)], ZL)

    def pass_r(k, half, name, row, to):
        u = sizes(k)[3]
        recv(k, "r1" + name)
        total = up32(r1[k, half, :, :u]) + up32(z1[k, row, :, half * u:half * u + u])
        r1[k, half, :, :u] = total.astype(BF)
        send("ra" + name, k, r1.at[k, half, :, pl.ds(0, u)], racc.at[k, half, :, pl.ds(0, u)], to)

    def finish(k):
        n = src_of(k)
        h, w, v, u = sizes(k)
        base = 3 * BASES[k % NP]
        recv(k, "yz", "ro+", "ro-", "ra+", "ra-")
        mine = zl * 4 + y
        F[:, :w] = (
            FY[k, 2 + zl, :, :w] + up32(yacc[k, zl, :, :w]) + up32(yown[k, zl, :, :w]) + up32(yz[k, :, :w])
        )
        for half in (0, 1):
            cols = slice(half * u, half * u + u)
            F[:, w + half * u:w + half * u + u] = (
                FZ[k, y, :, cols] + up32(z1[k, y, :, cols])
                + up32(racc[k, half, :, :u]) + up32(rown[k, half, :, :u])
            )
        gate, upper, back = F[:, :h], F[:, h:2 * h], F[:, 2 * h:3 * h]
        sigma = jax.nn.sigmoid(gate)
        swish = gate * sigma
        H[n, c, mine, :, base:base + h] = (swish * upper).astype(BF)
        H[n, c, mine, :, base + h:base + 2 * h] = (
            back * upper * sigma * (1.0 + gate * (1.0 - sigma))
        ).astype(BF)
        H[n, c, mine, :, base + 2 * h:base + 3 * h] = (back * swish).astype(BF)
        a = H.at[n, c, mine, :, y_cols(k)]
        b = H.at[n, c, mine, :, z_cols(k)]
        send("az", k, a, a, ZL)
        send("ay+", k, a, a, YP)
        send("ay-", k, a, a, YM)
        send("by+", k, b, b, YP)
        send("by-", k, b, b, YM)
        send("bz0", k, b, b, ZL)

    def move(name, k, plane, row, cols, to):
        part = H.at[src_of(k), c, plane * 4 + row, :, cols]
        send(name, k, part, part, to)

    def plus_b(k):
        recv(k, "by+")
        move("bf+", k, zl, ym, z_half(k, 0), YP)
        move("bz1", k, zl, ym, z_cols(k), ZL)

    def minus_b(k):
        recv(k, "by-")
        move("bf-", k, zl, yp, z_half(k, 1), YM)
        move("bz2", k, zl, yp, z_cols(k), ZL)

    def plane_a(k):
        recv(k, "az")
        move("ap+", k, oz, y, y_cols(k), YP)
        move("ap-", k, oz, y, y_cols(k), YM)

    def plus_a(k):
        recv(k, "ay+")
        move("af+", k, zl, ym, y_cols(k), YP)

    def far_b(k):
        recv(k, "bf+", "bf-")
        move("bz3", k, zl, y2, z_cols(k), ZL)

    def far_a(k):
        recv(k, "ap-")
        move("af-", k, oz, yp, y_cols(k), YM)

    def core_near(k):
        recv(k, "ay-")
        for n, row in enumerate((y, ym, yp)):
            move(f"ca{n}", k, zl, row, all_cols(k), CO)

    def core_far(k):
        recv(k, "af+", "af-", "ap+", "bz0", "bz1", "bz2", "bz3")
        part = H.at[src_of(k), c, pl.ds(oz * 4, 4), :, all_cols(k)]
        send("cc0", k, part, part, CO)
        move("cc1", k, zl, y2, all_cols(k), CO)

    def outputs(k):
        n, j = src_of(k), k % NP
        h = sizes(k)[0]
        base = 3 * BASES[j]
        hid = slice(BASES[j], BASES[j] + h)
        recv(k, "ca0", "ca1", "ca2", "cc0", "cc1")
        shape = (2, 2, 4, BIN, WIDTH)
        first = H[n, :, :, :, base:base + h].reshape(256, h)
        block = jnp.dot(first, wd[hid, :], preferred_element_type=F32).reshape(shape)
        first = H[n, :, :, :, base + h:base + 2 * h].reshape(256, h)
        inner = lax.dot_general(first, wg[:, hid], NT, preferred_element_type=F32)
        first = H[n, :, :, :, base + 2 * h:base + 3 * h].reshape(256, h)
        inner += lax.dot_general(first, wu[:, hid], NT, preferred_element_type=F32)
        inner = inner.reshape(shape)
        if j > 0:
            block += OB[n, :, :, :, :, :WIDTH]
            inner += OB[n, :, :, :, :, WIDTH:]
        OB[n, :, :, :, :, :WIDTH] = block
        OB[n, :, :, :, :, WIDTH:] = inner
        if j < NP - 1:
            return
        OL[n, :, :, :, :, :WIDTH] = block.astype(BF)
        OL[n, :, :, :, :, WIDTH:] = inner.astype(BF)
        if n < NS - 1:
            send("m+", n, OL.at[n, :, :, xp], rm.at[n], XP)
            send("m-", n, OL.at[n, :, :, xm], rp.at[n], XM)
            send("m2", n, OL.at[n, :, :, x2], r2.at[n], X2)
        else:
            send("dzx2", 0, OL.at[n, :, oh, x2], dr.at[6], dev(zh_=oh, x_=x2))
            send("dzx+", 0, OL.at[n, :, oh, xp], dr.at[4], dev(zh_=oh, x_=xp))
            send("dzx-", 0, OL.at[n, :, oh, xm], dr.at[5], dev(zh_=oh, x_=xm))
            send("dz", 0, OL.at[n, :, oh, x], dr.at[3], ZH)
            send("dx2", 0, OL.at[n, :, zh, x2], dr.at[2], X2)
            send("dx+", 0, OL.at[n, :, zh, xp], dr.at[0], XP)
            send("dx-", 0, OL.at[n, :, zh, xm], dr.at[1], XM)

    PLACES = ((0, 2, 1, 3), (2, 3, 0, 1), (3, 1, 2, 0), (1, 0, 3, 2))

    def earlier_sum(r, half):
        total = None
        for n, ref in zip(PLACES[r], (None, rm, rp, r2)):
            if n < NS - 1:
                part = OB[n, :, half, x] if ref is None else up32(ref[n, :, half])
                total = part if total is None else total + part
        return total

    def seq_exchange(k):
        for n in range(NS - 1):
            recv(n, "m+", "m-", "m2")
        for r in range(4):
            sz[r] = earlier_sum(r, oh).astype(BF)
        send("sz", 0, sz, rz, ZH)

    def seq_finish(k):
        recv(0, "dx+", "dx-", "dx2", "dz", "dzx+", "dzx-", "dzx2", "sz")
        late = {0: (2, 6), 1: (0, 4), 2: (3,), 3: (1, 5)}
        for r in range(4):
            total = earlier_sum(r, zh) + up32(rz[r])
            for j in late[r]:
                total += up32(dr[j])
            if r == 2:
                total += OB[NS - 1, :, zh, x]
            total = total.astype(BF)
            source = lax.rem(x + r, 4)
            block_out[:, source] = total[:, :, :WIDTH]
            input_out[:, source] = total[:, :, WIDTH:]

    def weight_grads(k):
        acts = G[0].reshape(1024, WIDTH)
        grads = G[1].reshape(1024, WIDTH)
        for j in range(NP):
            h = PARTS[j]
            for at in range(0, h, 512):
                width = min(512, h - at)
                to = pl.ds(BASES[j] + at, width)
                for place, out in ((1, tg), (2, tu)):
                    cols = pl.ds(3 * BASES[j] + place * h + at, width)
                    part = H[:, :, :, :, cols].reshape(1024, width)
                    part = lax.dot_general(acts, part, TN, preferred_element_type=F32)
                    out[:, to] = (part * (1.0 / 32.0)).astype(BF)
                part = H[:, :, :, :, pl.ds(3 * BASES[j] + at, width)].reshape(1024, width)
                part = lax.dot_general(part, grads, TN, preferred_element_type=F32)
                td[to, :] = (part * (1.0 / 32.0)).astype(BF)
        local_copy(tg, gate_out)
        local_copy(tu, up_out)
        local_copy(td, down_out)

    steps = {
        "pro": pack_acts, "pro2": pack_grads, "wl": swap_weights, "zha": peer_acts, "zhg": peer_grads,
        "sx": pass_on, "sy": far_rows, "fa": forward_y, "fb": forward_z,
        "ya+": lambda k: pass_y(k, 0, "+", YP), "ya-": lambda k: pass_y(k, 1, "-", YM),
        "zr": pass_z, "yz": cross_z,
        "ra+": lambda k: pass_r(k, 0, "+", yp, YP), "ra-": lambda k: pass_r(k, 1, "-", ym, YM),
        "fin": finish, "bp": plus_b, "bm": minus_b, "ap": plane_a, "af+": plus_a,
        "b3": far_b, "af-": far_a, "ca": core_near, "cc": core_far, "last": outputs,
        "sz": seq_exchange, "wgrad": weight_grads, "end": seq_finish,
    }
    for name, k in ORDER:
        steps[name](k)
    for cp in copies.values():
        cp.wait_send()
    for cp in local[len(loads):]:
        cp.wait()


def run_mega(acts, grads, lengths, dest, mask, adv, gate, up, down):
    vm = pltpu.VMEM
    shape = jax.ShapeDtypeStruct
    rows = shape((2, 4, BIN, WIDTH), BF)
    wide, tall = shape((WIDTH, HID), BF), shape((HID, WIDTH), BF)
    hbm = pl.BlockSpec(memory_space=pl.ANY)
    whole = pl.BlockSpec(memory_space=vm)
    late = vm((NS - 1, 2, 2, BIN, 2 * WIDTH), BF)
    ybuf, zbuf = vm((NK, 2, BIN, MAXY), BF), vm((NK, 2, BIN, MAXZ // 2), BF)
    return pl.pallas_call(
        mega,
        out_shape=(rows, rows, wide, wide, tall),
        in_specs=[whole] * 6 + [hbm] * 3,
        out_specs=(whole, whole, hbm, hbm, hbm),
        scratch_shapes=[
            vm((WIDTH, HID), BF), vm((WIDTH, HID), BF), vm((HID, WIDTH), BF),
            vm((WIDTH, HID), BF), vm((WIDTH, HID), BF), vm((HID, WIDTH), BF),
            vm((2, NS, 2, 128, WIDTH), BF),
            vm((2, NS, 128, WIDTH), BF),
            vm((NK, 4, BIN, MAXY), BF), vm((NK, 4, BIN, MAXZ), BF),
            vm((NK, 4, BIN, MAXY), F32), vm((NK, 4, BIN, MAXZ), F32),
            vm((NS, 2, 8, BIN, ALL), BF),
            ybuf, ybuf, ybuf,
            vm((NK, BIN, MAXY), BF), vm((NK, BIN, MAXY), BF),
            vm((NK, 4, BIN, MAXZ), BF),
            zbuf, zbuf, zbuf,
            vm((BIN, 3 * max(PARTS)), F32),
            vm((NS, 2, 2, 4, BIN, 2 * WIDTH), F32),
            vm((NS, 2, 2, 4, BIN, 2 * WIDTH), BF),
            late, late, late,
            vm((4, 2, BIN, 2 * WIDTH), BF), vm((4, 2, BIN, 2 * WIDTH), BF),
            vm((7, 2, BIN, 2 * WIDTH), BF),
            vm((WIDTH, HID), BF), vm((WIDTH, HID), BF), vm((HID, WIDTH), BF),
            pltpu.SemaphoreType.DMA((N_SEM,)),
            pltpu.SemaphoreType.DMA((N_SEM,)),
            pltpu.SemaphoreType.DMA((8,)),
        ],
        compiler_params=pltpu.CompilerParams(
            collective_id=0, has_side_effects=True, vmem_limit_bytes=62 * 2**20
        ),
        name="mega",
    )(acts, grads, lengths, dest, mask, adv, gate, up, down)


def per_device(
    rollout_acts, rollout_grads, lengths, destination, valid_mask, advantage,
    gate_weight, up_weight, down_weight,
):
    block, inner, gate_grad, up_grad, down_grad = run_mega(
        rollout_acts, rollout_grads, lengths, destination, valid_mask[None, :], advantage,
        gate_weight, up_weight, down_weight,
    )
    return (
        block.reshape(128, WIDTH), inner.reshape(128, WIDTH),
        gate_grad.astype(F32), up_grad.astype(F32), down_grad.astype(F32),
    )


def solution(mesh):
    return jax.shard_map(
        per_device,
        mesh=mesh,
        in_specs=(
            P("seq", "tp"), P("seq", "tp"), P("seq", None), P("seq", None), P("seq"),
            P("seq", None), P("tp", "seq"), P("tp", "seq"), P("seq", "tp"),
        ),
        out_specs=(P("seq", "tp"), P("seq", "tp"), P("tp", "seq"), P("tp", "seq"), P("seq", "tp")),
        check_vma=False,
    )
```

time: 157 us -> 134 us (0.85)
  Pallas kernels: 146 us -> 123 us
    pallas_call x1, Pallas kernels: 146 us -> 123 us  [run_mega(): pl.pallas_call(mega, out_shape=(rows, rows, wide, wide, tall), in_specs=[...]
where the time goes in v3:
time: 134 us
  Pallas kernels  123 us (92%)
  other arithmetic  8.55 us (6%)
  local copies, waits for them, and re-layouts  1.43 us (1%)
    pallas_call x1, Pallas kernels, run_mega(): pl.pallas_call(mega, out_shape=(rows, rows, wide, wide, tall), in_specs=[...  123 us
    convert_element_type x1, other arithmetic, per_device(): gate_grad.astype(F32)  3.88 us

profile of v3, /device:TPU:0, one launch (start us, length us, event | category | flops | bytes accessed | tf_op | source)
XLA Modules:
  0.0 133.7 jit_solution(8110021218037342373)
XLA Ops:
  0.6 123.1 %mega.1 = (bf16[2,4,16,512]{3,2,1,0:T(8,128)(2,1)}, bf16[2,4,16,512]{3,2,1,0:T(8,128)(2,1)}, bf16[512,1920]{1,0:T(8,128)(2,1)}, bf16[512,1920]{1,0:T(8,128)(2,1)}, bf16[1920,512]{1,0:T(8,128)(2,1)}) custom-call(bf16[256,512]{1,0:T(8,128)(2,1)} %acts_ref.1, bf16[256,512]{1,0:T(8,128)(2,1)} %grads_ref.1, s32[1,16]{1,0:T(1,128)} %lengths_ref.1, ...), custom_call_target="tpu_custom_call" | custom-call | tf_op jit(solution)/shard_map/mega/pallas_call | solution.py:485
  123.7 0.0 copy-start.1
  123.7 3.9 %convert_element_type.9 = f32[512,1920]{1,0:T(8,128)} convert(bf16[512,1920]{1,0:T(8,128)(2,1)} %get-tuple-element.12) | non-fusion elementwise | flops 983040 | bytes 5898240 | tf_op jit(solution)/shard_map/convert_element_type | solution.py:530
  127.6 0.0 copy-done.1
  127.6 0.0 copy-start
  127.6 2.2 %convert_element_type.10 = f32[512,1920]{1,0:T(8,128)} convert(bf16[512,1920]{1,0:T(8,128)(2,1)S(1)} %copy-done.1) | non-fusion elementwise | flops 983040 | bytes 5898240 | tf_op jit(solution)/shard_map/convert_element_type | solution.py:530
  129.8 0.1 copy-done
  129.9 0.0 copy-start.3
  129.9 0.0 copy-start.2
  129.9 2.5 %convert_element_type.11 = f32[1920,512]{1,0:T(8,128)} convert(bf16[1920,512]{1,0:T(8,128)(2,1)S(1)} %copy-done) | non-fusion elementwise | flops 983040 | bytes 5898240 | tf_op jit(solution)/shard_map/convert_element_type | solution.py:530
  132.4 0.0 copy-done.3
  132.4 0.7 copy.16
  133.1 0.0 copy-done.2
  133.1 0.7 copy.17
Async XLA Ops:
  123.7 3.9 %copy-start.1 = (bf16[512,1920]{1,0:T(8,128)(2,1)S(1)}, bf16[512,1920]{1,0:T(8,128)(2,1)}, u32[]{:S(2)}) copy-start(bf16[512,1920]{1,0:T(8,128)(2,1)} %get-tuple-element.13) | copy-start | bytes 5898244
  127.6 2.3 %copy-start = (bf16[1920,512]{1,0:T(8,128)(2,1)S(1)}, bf16[1920,512]{1,0:T(8,128)(2,1)}, u32[]{:S(2)}) copy-start(bf16[1920,512]{1,0:T(8,128)(2,1)} %get-tuple-element.14) | copy-start | bytes 5898244
  129.9 2.5 %copy-start.3 = (bf16[2,4,16,512]{3,2,1,0:T(8,128)(2,1)S(1)}, bf16[2,4,16,512]{3,2,1,0:T(8,128)(2,1)}, u32[]{:S(2)}) copy-start(bf16[2,4,16,512]{3,2,1,0:T(8,128)(2,1)} %get-tuple-element.10) | copy-start | bytes 393220
  129.9 3.1 %copy-start.2 = (bf16[2,4,16,512]{3,2,1,0:T(8,128)(2,1)S(1)}, bf16[2,4,16,512]{3,2,1,0:T(8,128)(2,1)}, u32[]{:S(2)}) copy-start(bf16[2,4,16,512]{3,2,1,0:T(8,128)(2,1)} %get-tuple-element.11) | copy-start | bytes 393220

commit v4 on v3

--- a/solution.py
+++ b/solution.py
@@ -9,8 +9,8 @@
 NS = 4
 WIDTH = 512
 HID = 1920
-PARTS = (1920,)
-YCOLS = (3456,)
+PARTS = (1024, 896)
+YCOLS = (1792, 1664)
 NP = len(PARTS)
 NK = NS * NP
 BASES = tuple(sum(PARTS[:j]) for j in range(NP))
@@ -24,16 +24,14 @@
 TN = (((0,), (0,)), ((), ()))
 
 ORDER = (
-    ("pro", 0), ("pro2", 0), ("wl", 0), ("zha", 0), ("zhg", 0), ("fa", 0), ("fb", 0), ("sx", 0), ("ya+", 0),
-    ("ya-", 0), ("fa", 1), ("fb", 1), ("yz", 0), ("sy", 0), ("zr", 0), ("fa", 2), ("ya+", 1), ("ya-", 1),
-    ("fb", 2), ("ra+", 0), ("ra-", 0), ("zr", 1), ("ya+", 2), ("ya-", 2), ("yz", 1), ("fin", 0), ("ra+", 1),
-    ("ra-", 1), ("zr", 2), ("yz", 2), ("ap", 0), ("af+", 0), ("bp", 0), ("bm", 0), ("ca", 0), ("fin", 1),
-    ("ra+", 2), ("ra-", 2), ("af-", 0), ("ap", 1), ("b3", 0), ("fa", 3), ("bm", 1), ("af+", 1), ("fb", 3),
-    ("bp", 1), ("ca", 1), ("fin", 2), ("cc", 0), ("af-", 1), ("last", 0), ("ya+", 3), ("ya-", 3), ("zr", 3),
-    ("b3", 1), ("ap", 2), ("bm", 2), ("af+", 2), ("bp", 2), ("cc", 1), ("ca", 2), ("yz", 3), ("ra+", 3),
-    ("ra-", 3), ("last", 1), ("af-", 2), ("b3", 2), ("fin", 3), ("cc", 2), ("af+", 3), ("ap", 3),
-    ("last", 2), ("bp", 3), ("bm", 3), ("ca", 3), ("af-", 3), ("b3", 3), ("sz", 0), ("cc", 3), ("last", 3),
-    ("wgrad", 0), ("end", 0),
+    0, 10, 20, 30, 40, 70, 80, 71, 50, 81, 90, 100, 72, 82, 91, 101, 110, 120, 111, 92, 102, 60, 73, 83,
+    130, 140, 121, 131, 141, 112, 74, 122, 84, 93, 103, 113, 150, 151, 132, 142, 94, 104, 123, 133, 143,
+    114, 180, 190, 160, 170, 220, 181, 191, 161, 171, 221, 152, 124, 153, 134, 144, 210, 182, 200, 211, 75,
+    85, 172, 201, 183, 192, 173, 162, 222, 193, 230, 163, 223, 154, 212, 115, 231, 240, 95, 105, 241, 213,
+    184, 202, 174, 203, 194, 232, 145, 164, 224, 135, 76, 125, 233, 86, 214, 77, 87, 204, 242, 155, 96, 106,
+    243, 116, 97, 107, 195, 117, 165, 234, 175, 225, 126, 136, 185, 146, 244, 127, 137, 147, 205, 215, 156,
+    157, 235, 186, 196, 166, 176, 226, 245, 187, 197, 167, 177, 227, 216, 206, 217, 207, 236, 250, 246, 237,
+    247, 260, 270,
 )
 
 SEQ_NAMES = (
@@ -93,10 +91,10 @@
 
 def mega(
     acts_ref, grads_ref, lengths_ref, dest_ref, mask_ref, adv_ref, gate_hbm, up_hbm, down_hbm,
-    block_out, input_out, gate_out, up_out, down_out,
+    block_out, input_out, tg, tu, td,
     wg, wu, wd, pg, pu, pd, G, Q, RY, RZ, FY, FZ, H,
     y1, yown, yacc, ysend, yz, z1, r1, rown, racc, F,
-    OB, OL, rm, rp, r2, sz, rz, dr, tg, tu, td,
+    OB, OL, rm, rp, r2, sz, rz, dr,
     ssem, rsem, lsem,
 ):
     s = lax.axis_index("seq")
@@ -162,7 +160,6 @@
     loads = [local_copy(gate_hbm, wg), local_copy(up_hbm, wu), local_copy(down_hbm, wd)]
     barrier = pltpu.get_barrier_semaphore()
     peers = [XP, XM, YP, YM, ZL, ZH, CO, X2]
-    peers += [dev(zh_=oh, x_=x_) for x_ in (xp, xm, x2)]
     for peer in peers:
         pl.semaphore_signal(barrier, inc=1, device_id=peer, device_id_type=MESH)
     hot, weight = routing(lengths_ref[...], dest_ref[...], adv_ref[...], mask_ref[...])
@@ -269,6 +266,12 @@
         y1[k, half, :, :w] = (up32(y1[k, half, :, :w]) + FY[k, half, :, :w]).astype(BF)
         send("ya" + name, k, y1.at[k, half, :, pl.ds(0, w)], yacc.at[k, half, :, pl.ds(0, w)], to)
 
+    def plus_y(k):
+        pass_y(k, 0, "+", YP)
+
+    def minus_y(k):
+        pass_y(k, 1, "-", YM)
+
     def pass_z(k):
         _, _, v, u = sizes(k)
         recv(k, "z1")
@@ -293,6 +296,12 @@
         total = up32(r1[k, half, :, :u]) + up32(z1[k, row, :, half * u:half * u + u])
         r1[k, half, :, :u] = total.astype(BF)
         send("ra" + name, k, r1.at[k, half, :, pl.ds(0, u)], racc.at[k, half, :, pl.ds(0, u)], to)
+
+    def plus_r(k):
+        pass_r(k, 0, "+", yp, YP)
+
+    def minus_r(k):
+        pass_r(k, 1, "-", ym, YM)
 
     def finish(k):
         n = src_of(k)
@@ -451,33 +460,24 @@
                 part = H[:, :, :, :, pl.ds(3 * BASES[j] + at, width)].reshape(1024, width)
                 part = lax.dot_general(part, grads, TN, preferred_element_type=F32)
                 td[to, :] = (part * (1.0 / 32.0)).astype(BF)
-        local_copy(tg, gate_out)
-        local_copy(tu, up_out)
-        local_copy(td, down_out)
-
-    steps = {
-        "pro": pack_acts, "pro2": pack_grads, "wl": swap_weights, "zha": peer_acts, "zhg": peer_grads,
-        "sx": pass_on, "sy": far_rows, "fa": forward_y, "fb": forward_z,
-        "ya+": lambda k: pass_y(k, 0, "+", YP), "ya-": lambda k: pass_y(k, 1, "-", YM),
-        "zr": pass_z, "yz": cross_z,
-        "ra+": lambda k: pass_r(k, 0, "+", yp, YP), "ra-": lambda k: pass_r(k, 1, "-", ym, YM),
-        "fin": finish, "bp": plus_b, "bm": minus_b, "ap": plane_a, "af+": plus_a,
-        "b3": far_b, "af-": far_a, "ca": core_near, "cc": core_far, "last": outputs,
-        "sz": seq_exchange, "wgrad": weight_grads, "end": seq_finish,
-    }
-    for name, k in ORDER:
-        steps[name](k)
+
+    steps = (
+        pack_acts, pack_grads, swap_weights, peer_acts, peer_grads, pass_on, far_rows,
+        forward_y, forward_z, plus_y, minus_y, pass_z, cross_z, plus_r, minus_r, finish,
+        plus_b, minus_b, plane_a, plus_a, far_b, far_a, core_near, core_far, outputs,
+        seq_exchange, weight_grads, seq_finish,
+    )
+    for step in ORDER:
+        steps[step // 10](step % 10)
     for cp in copies.values():
         cp.wait_send()
-    for cp in local[len(loads):]:
-        cp.wait()
 
 
 def run_mega(acts, grads, lengths, dest, mask, adv, gate, up, down):
     vm = pltpu.VMEM
     shape = jax.ShapeDtypeStruct
-    rows = shape((2, 4, BIN, WIDTH), BF)
-    wide, tall = shape((WIDTH, HID), BF), shape((HID, WIDTH), BF)
+    rows = vm((2, 4, BIN, WIDTH), BF)
+    wide, tall = vm((WIDTH, HID), BF), vm((HID, WIDTH), BF)
     hbm = pl.BlockSpec(memory_space=pl.ANY)
     whole = pl.BlockSpec(memory_space=vm)
     late = vm((NS - 1, 2, 2, BIN, 2 * WIDTH), BF)
@@ -486,7 +486,7 @@
         mega,
         out_shape=(rows, rows, wide, wide, tall),
         in_specs=[whole] * 6 + [hbm] * 3,
-        out_specs=(whole, whole, hbm, hbm, hbm),
+        out_specs=(whole,) * 5,
         scratch_shapes=[
             vm((WIDTH, HID), BF), vm((WIDTH, HID), BF), vm((HID, WIDTH), BF),
             vm((WIDTH, HID), BF), vm((WIDTH, HID), BF), vm((HID, WIDTH), BF),
@@ -505,16 +505,56 @@
             late, late, late,
             vm((4, 2, BIN, 2 * WIDTH), BF), vm((4, 2, BIN, 2 * WIDTH), BF),
             vm((7, 2, BIN, 2 * WIDTH), BF),
-            vm((WIDTH, HID), BF), vm((WIDTH, HID), BF), vm((HID, WIDTH), BF),
             pltpu.SemaphoreType.DMA((N_SEM,)),
             pltpu.SemaphoreType.DMA((N_SEM,)),
             pltpu.SemaphoreType.DMA((8,)),
         ],
         compiler_params=pltpu.CompilerParams(
-            collective_id=0, has_side_effects=True, vmem_limit_bytes=62 * 2**20
+            collective_id=0, has_side_effects=True, vmem_limit_bytes=54 * 2**20
         ),
         name="mega",
     )(acts, grads, lengths, dest, mask, adv, gate, up, down)
+
+
+def widen_kernel(
+    block, inner, wide_a, wide_b, tall, out_block, out_inner, out_a, out_b, out_c, stage, stage_tall, sem
+):
+    small = [
+        pltpu.make_async_copy(block, out_block, sem.at[4]), pltpu.make_async_copy(inner, out_inner, sem.at[5])
+    ]
+    for cp in small:
+        cp.start()
+    pieces = [(src, dst, at, 128, stage) for src, dst in ((wide_a, out_a), (wide_b, out_b)) for at in range(0, WIDTH, 128)]
+    pieces += [(tall, out_c, at, 480, stage_tall) for at in range(0, HID, 480)]
+    flying = []
+    for n, (src, dst, at, rows, held) in enumerate(pieces):
+        slot = n % 4
+        if n >= 4:
+            flying[n - 4].wait()
+        held[slot] = up32(src[at:at + rows, :])
+        cp = pltpu.make_async_copy(held.at[slot], dst.at[pl.ds(at, rows)], sem.at[slot])
+        cp.start()
+        flying.append(cp)
+    for cp in flying[-4:] + small:
+        cp.wait()
+
+
+def widen(block, inner, wide_a, wide_b, tall):
+    shape = jax.ShapeDtypeStruct
+    return pl.pallas_call(
+        widen_kernel,
+        out_shape=(
+            shape(block.shape, BF), shape(inner.shape, BF),
+            shape((WIDTH, HID), F32), shape((WIDTH, HID), F32), shape((HID, WIDTH), F32),
+        ),
+        in_specs=[pl.BlockSpec(memory_space=pltpu.VMEM)] * 5,
+        out_specs=(pl.BlockSpec(memory_space=pl.ANY),) * 5,
+        scratch_shapes=[
+            pltpu.VMEM((4, 128, HID), F32), pltpu.VMEM((4, 480, WIDTH), F32), pltpu.SemaphoreType.DMA((6,)),
+        ],
+        compiler_params=pltpu.CompilerParams(vmem_limit_bytes=12 * 2**20),
+        name="widen",
+    )(block, inner, wide_a, wide_b, tall)
 
 
 def per_device(
@@ -525,10 +565,7 @@
         rollout_acts, rollout_grads, lengths, destination, valid_mask[None, :], advantage,
         gate_weight, up_weight, down_weight,
     )
-    return (
-        block.reshape(128, WIDTH), inner.reshape(128, WIDTH),
-        gate_grad.astype(F32), up_grad.astype(F32), down_grad.astype(F32),
-    )
+    return widen(block.reshape(128, WIDTH), inner.reshape(128, WIDTH), gate_grad, up_grad, down_grad)
 
 
 def solution(mesh):

time: 134 us -> 126 us (0.940)
  other arithmetic: 8.55 us -> 0 us
  local copies, waits for them, and re-layouts: 1.43 us -> 0 us
    convert_element_type x3 -> x0, other arithmetic: 8.55 us -> none  [the longest x1 3.88 us: per_device(): gate_grad.astype(F32)]
    pallas_call x0 -> x1, Pallas kernels: none -> 4.45 us  [widen(): pl.pallas_call(widen_kernel, out_shape=(shape(block.shape, BF), shape(inn...]
    pallas_call x1, Pallas kernels: 123 us -> 120 us  [run_mega(): pl.pallas_call(mega, out_shape=(rows, rows, wide, wide, tall), in_specs=[...]
    unnamed x10 -> x0, local copies, waits for them, and re-layouts: 1.43 us -> none
where the time goes in v4:
time: 126 us; the launch traced here: 125 us
  Pallas kernels  124 us (98%)
    pallas_call x1, Pallas kernels, run_mega(): pl.pallas_call(mega, out_shape=(rows, rows, wide, wide, tall), in_specs=[...  120 us
    pallas_call x1, Pallas kernels, widen(): pl.pallas_call(widen_kernel, out_shape=(shape(block.shape, BF), shape(inn...  4.45 us

profile of v4, /device:TPU:0, one launch (start us, length us, event | category | flops | bytes accessed | tf_op | source)
XLA Modules:
  0.0 124.9 jit_solution(6994358078130493110)
XLA Ops:
  0.6 119.6 %mega.1 = (bf16[2,4,16,512]{3,2,1,0:T(8,128)(2,1)S(1)}, bf16[2,4,16,512]{3,2,1,0:T(8,128)(2,1)S(1)}, bf16[512,1920]{1,0:T(8,128)(2,1)S(1)}, bf16[512,1920]{1,0:T(8,128)(2,1)S(1)}, bf16[1920,512]{1,0:T(8,128)(2,1)S(1)}) custom-call(bf16[256,512]{1,0:T(8,128)(2,1)} %acts_ref.1, bf16[256,512]{1,0:T(8,128)(2,1)} %grads_ref.1, s32[1,16]{1,0:T(1,128)} %lengths_ref.1, ...), custom_call_target="tpu_custom_call" | custom-call | tf_op jit(solution)/shard_map/mega/pallas_call | solution.py:485
  120.3 4.4 %widen.1 = (bf16[128,512]{1,0:T(8,128)(2,1)}, bf16[128,512]{1,0:T(8,128)(2,1)}, f32[512,1920]{1,0:T(8,128)}, f32[512,1920]{1,0:T(8,128)}, f32[1920,512]{1,0:T(8,128)}) custom-call(bf16[128,512]{1,0:T(8,128)(2,1)S(1)} %bitcast.3, bf16[128,512]{1,0:T(8,128)(2,1)S(1)} %bitcast.4, bf16[512,1920]{1,0:T(8,128)(2,1)S(1)} %get-tuple-element.12.wide_a, ...), custom_call_target="tpu_custom_call" | custom-call | tf_op jit(solution)/shard_map/widen/pallas_call | solution.py:544

commit v5 on v4

--- a/solution.py
+++ b/solution.py
@@ -10,13 +10,14 @@
 WIDTH = 512
 HID = 1920
 PARTS = (1024, 896)
-YCOLS = (1792, 1664)
+YCOLS = (1792, 1664, 1792, 1664, 1280, 896, 1792, 1408)
+ACOLS = (1792, 2176, 1536, 1664, 1792, 1152, 1024, 2432)
 NP = len(PARTS)
 NK = NS * NP
 BASES = tuple(sum(PARTS[:j]) for j in range(NP))
 ALL = 3 * HID
 MAXY = max(YCOLS)
-MAXZ = max(3 * h - w for h, w in zip(PARTS, YCOLS))
+MAXZ = max(3 * PARTS[k % NP] - w for k, w in enumerate(YCOLS))
 BF = jnp.bfloat16
 F32 = jnp.float32
 MESH = pl.DeviceIdType.MESH
@@ -24,20 +25,21 @@
 TN = (((0,), (0,)), ((), ()))
 
 ORDER = (
-    0, 10, 20, 30, 40, 70, 80, 71, 50, 81, 90, 100, 72, 82, 91, 101, 110, 120, 111, 92, 102, 60, 73, 83,
-    130, 140, 121, 131, 141, 112, 74, 122, 84, 93, 103, 113, 150, 151, 132, 142, 94, 104, 123, 133, 143,
-    114, 180, 190, 160, 170, 220, 181, 191, 161, 171, 221, 152, 124, 153, 134, 144, 210, 182, 200, 211, 75,
-    85, 172, 201, 183, 192, 173, 162, 222, 193, 230, 163, 223, 154, 212, 115, 231, 240, 95, 105, 241, 213,
-    184, 202, 174, 203, 194, 232, 145, 164, 224, 135, 76, 125, 233, 86, 214, 77, 87, 204, 242, 155, 96, 106,
-    243, 116, 97, 107, 195, 117, 165, 234, 175, 225, 126, 136, 185, 146, 244, 127, 137, 147, 205, 215, 156,
-    157, 235, 186, 196, 166, 176, 226, 245, 187, 197, 167, 177, 227, 216, 206, 217, 207, 236, 250, 246, 237,
+    0, 10, 20, 30, 40, 70, 80, 71, 81, 50, 100, 90, 72, 82, 110, 73, 83, 120, 111, 74, 60, 84, 101, 130,
+    140, 112, 102, 91, 131, 141, 103, 92, 93, 104, 113, 94, 132, 150, 121, 142, 122, 75, 114, 85, 180, 123,
+    124, 133, 143, 190, 151, 170, 152, 160, 220, 105, 134, 144, 95, 210, 115, 171, 191, 153, 161, 172, 221,
+    181, 200, 162, 154, 182, 192, 222, 125, 135, 145, 173, 193, 183, 163, 201, 223, 211, 202, 230, 174, 194,
+    212, 164, 184, 224, 240, 213, 155, 231, 76, 232, 203, 86, 214, 77, 204, 185, 87, 241, 233, 175, 165,
+    106, 195, 225, 96, 242, 116, 234, 107, 97, 243, 205, 215, 244, 117, 126, 136, 146, 127, 235, 137, 147,
+    156, 157, 245, 186, 196, 166, 176, 226, 187, 177, 167, 216, 197, 227, 206, 217, 207, 250, 236, 237, 246,
     247, 260, 270,
 )
 
 SEQ_NAMES = (
     "zha", "zhg", "xoa+", "xoa-", "xog+", "xog-", "xpa+", "xpa-", "xpg+", "xpg-", "xf+", "xf-",
-    "sz", "dx+", "dx-", "dx2", "dz", "dzx+", "dzx-", "dzx2",
+    "sz",
 )
+LATE_NAMES = ("dx+", "dx-", "dx2", "dz", "dzx+", "dzx-", "dzx2")
 PIECE_NAMES = (
     "y1+", "y1-", "yo+", "yo-", "ya+", "ya-", "yz",
     "z1", "r1+", "r1-", "ro+", "ro-", "ra+", "ra-",
@@ -47,6 +49,9 @@
 SEM = {}
 for _n in SEQ_NAMES:
     SEM[(_n, 0)] = len(SEM)
+for _k in range(2):
+    for _n in LATE_NAMES:
+        SEM[(_n, _k)] = len(SEM)
 for _k in range(NP):
     for _n in ("wg", "wu", "wd"):
         SEM[(_n, _k)] = len(SEM)
@@ -90,9 +95,9 @@
 
 
 def mega(
-    acts_ref, grads_ref, lengths_ref, dest_ref, mask_ref, adv_ref, gate_hbm, up_hbm, down_hbm,
+    acts_hbm, grads_hbm, lengths_ref, dest_ref, mask_ref, adv_ref, gate_hbm, up_hbm, down_hbm,
     block_out, input_out, tg, tu, td,
-    wg, wu, wd, pg, pu, pd, G, Q, RY, RZ, FY, FZ, H,
+    acts_ref, grads_ref, wg, wu, wd, pg, pu, pd, G, Q, RY, RZ, FY, FZ, H,
     y1, yown, yacc, ysend, yz, z1, r1, rown, racc, F,
     OB, OL, rm, rp, r2, sz, rz, dr,
     ssem, rsem, lsem,
@@ -142,26 +147,28 @@
         return pl.ds(BASES[k % NP], PARTS[k % NP])
 
     def sizes(k):
-        h, w = PARTS[k % NP], YCOLS[k % NP]
+        h, w = PARTS[k % NP], YCOLS[k]
         return h, w, 3 * h - w, (3 * h - w) // 2
 
     def all_cols(k):
         return pl.ds(3 * BASES[k % NP], 3 * PARTS[k % NP])
 
     def y_cols(k):
-        return pl.ds(3 * BASES[k % NP], YCOLS[k % NP])
+        return pl.ds(3 * BASES[k % NP], ACOLS[k])
 
     def z_cols(k):
-        return pl.ds(3 * BASES[k % NP] + YCOLS[k % NP], sizes(k)[2])
+        return pl.ds(3 * BASES[k % NP] + ACOLS[k], 3 * PARTS[k % NP] - ACOLS[k])
 
     def z_half(k, half):
-        return pl.ds(3 * BASES[k % NP] + YCOLS[k % NP] + half * sizes(k)[3], sizes(k)[3])
-
-    loads = [local_copy(gate_hbm, wg), local_copy(up_hbm, wu), local_copy(down_hbm, wd)]
+        width = (3 * PARTS[k % NP] - ACOLS[k]) // 2
+        return pl.ds(3 * BASES[k % NP] + ACOLS[k] + half * width, width)
+
     barrier = pltpu.get_barrier_semaphore()
     peers = [XP, XM, YP, YM, ZL, ZH, CO, X2]
     for peer in peers:
         pl.semaphore_signal(barrier, inc=1, device_id=peer, device_id_type=MESH)
+    raw = [local_copy(acts_hbm, acts_ref), local_copy(grads_hbm, grads_ref)]
+    loads = [local_copy(gate_hbm, wg), local_copy(up_hbm, wu), local_copy(down_hbm, wd)]
     hot, weight = routing(lengths_ref[...], dest_ref[...], adv_ref[...], mask_ref[...])
 
     def spread_own(arr, n):
@@ -176,11 +183,13 @@
         send("xp" + n + "-", 0, G.at[arr, 0, oh], G.at[arr, 2, oh], XM)
 
     def pack_acts(k):
+        raw[0].wait()
         G[0, 0, zh] = jnp.dot(hot, acts_ref[...], preferred_element_type=F32).astype(BF)
         pl.semaphore_wait(barrier, len(peers))
         spread_own(0, "a")
 
     def pack_grads(k):
+        raw[1].wait()
         packed = jnp.dot(hot, grads_ref[...], preferred_element_type=F32)
         G[1, 0, zh] = (packed * weight).astype(BF)
         spread_own(1, "g")
@@ -238,8 +247,9 @@
         a, b = rows_in(G, (0, n, c), Y_ORDER), rows_in(Q, (0, n), Y_ORDER)
         cols = slice(base, base + h)
         keep(RY, FY, k, 0, product(a, b, wg[:, cols], pg[:, cols]))
-        cols = slice(base, base + w - h)
-        keep(RY, FY, k, h, product(a, b, wu[:, cols], pu[:, cols]))
+        if w > h:
+            cols = slice(base, base + w - h)
+            keep(RY, FY, k, h, product(a, b, wu[:, cols], pu[:, cols]))
         send("y1+", k, RY.at[k, 0, :, pl.ds(0, w)], y1.at[k, 0, :, pl.ds(0, w)], YP)
         send("y1-", k, RY.at[k, 1, :, pl.ds(0, w)], y1.at[k, 1, :, pl.ds(0, w)], YM)
         send("yo+", k, RY.at[k, 2, :, pl.ds(0, w)], yown.at[k, 1, :, pl.ds(0, w)], YP)
@@ -386,32 +396,38 @@
         shape = (2, 2, 4, BIN, WIDTH)
         first = H[n, :, :, :, base:base + h].reshape(256, h)
         block = jnp.dot(first, wd[hid, :], preferred_element_type=F32).reshape(shape)
+        if j > 0:
+            block += OB[n, :, :, :, :, :WIDTH]
+        OB[n, :, :, :, :, :WIDTH] = block
+        if j == NP - 1:
+            OL[n, :, :, :, :, :WIDTH] = block.astype(BF)
+            if n == NS - 1:
+                late_sends(0)
         first = H[n, :, :, :, base + h:base + 2 * h].reshape(256, h)
         inner = lax.dot_general(first, wg[:, hid], NT, preferred_element_type=F32)
         first = H[n, :, :, :, base + 2 * h:base + 3 * h].reshape(256, h)
         inner += lax.dot_general(first, wu[:, hid], NT, preferred_element_type=F32)
         inner = inner.reshape(shape)
         if j > 0:
-            block += OB[n, :, :, :, :, :WIDTH]
             inner += OB[n, :, :, :, :, WIDTH:]
-        OB[n, :, :, :, :, :WIDTH] = block
         OB[n, :, :, :, :, WIDTH:] = inner
         if j < NP - 1:
             return
-        OL[n, :, :, :, :, :WIDTH] = block.astype(BF)
         OL[n, :, :, :, :, WIDTH:] = inner.astype(BF)
         if n < NS - 1:
             send("m+", n, OL.at[n, :, :, xp], rm.at[n], XP)
             send("m-", n, OL.at[n, :, :, xm], rp.at[n], XM)
             send("m2", n, OL.at[n, :, :, x2], r2.at[n], X2)
         else:
-            send("dzx2", 0, OL.at[n, :, oh, x2], dr.at[6], dev(zh_=oh, x_=x2))
-            send("dzx+", 0, OL.at[n, :, oh, xp], dr.at[4], dev(zh_=oh, x_=xp))
-            send("dzx-", 0, OL.at[n, :, oh, xm], dr.at[5], dev(zh_=oh, x_=xm))
-            send("dz", 0, OL.at[n, :, oh, x], dr.at[3], ZH)
-            send("dx2", 0, OL.at[n, :, zh, x2], dr.at[2], X2)
-            send("dx+", 0, OL.at[n, :, zh, xp], dr.at[0], XP)
-            send("dx-", 0, OL.at[n, :, zh, xm], dr.at[1], XM)
+            late_sends(1)
+
+    def late_sends(side):
+        cols = pl.ds(side * WIDTH, WIDTH)
+        for name, slot, a, b in (
+            ("dzx2", 6, oh, x2), ("dzx+", 4, oh, xp), ("dzx-", 5, oh, xm), ("dz", 3, oh, x),
+            ("dx2", 2, zh, x2), ("dx+", 0, zh, xp), ("dx-", 1, zh, xm),
+        ):
+            send(name, side, OL.at[NS - 1, :, a, b, :, cols], dr.at[slot, :, :, cols], dev(zh_=a, x_=b))
 
     PLACES = ((0, 2, 1, 3), (2, 3, 0, 1), (3, 1, 2, 0), (1, 0, 3, 2))
 
@@ -431,7 +447,9 @@
         send("sz", 0, sz, rz, ZH)
 
     def seq_finish(k):
-        recv(0, "dx+", "dx-", "dx2", "dz", "dzx+", "dzx-", "dzx2", "sz")
+        recv(0, "sz")
+        for side in (0, 1):
+            recv(side, *LATE_NAMES)
         late = {0: (2, 6), 1: (0, 4), 2: (3,), 3: (1, 5)}
         for r in range(4):
             total = earlier_sum(r, zh) + up32(rz[r])
@@ -485,9 +503,10 @@
     return pl.pallas_call(
         mega,
         out_shape=(rows, rows, wide, wide, tall),
-        in_specs=[whole] * 6 + [hbm] * 3,
+        in_specs=[hbm] * 2 + [whole] * 4 + [hbm] * 3,
         out_specs=(whole,) * 5,
         scratch_shapes=[
+            vm((2 * 128, WIDTH), BF), vm((2 * 128, WIDTH), BF),
             vm((WIDTH, HID), BF), vm((WIDTH, HID), BF), vm((HID, WIDTH), BF),
             vm((WIDTH, HID), BF), vm((WIDTH, HID), BF), vm((HID, WIDTH), BF),
             vm((2, NS, 2, 128, WIDTH), BF),

time: 126 us -> 124 us (0.984); the launches traced: 125 us -> 122 us
  Pallas kernels: 124 us -> 121 us
    pallas_call x1, Pallas kernels: 120 us -> 116 us  [run_mega(): pl.pallas_call(mega, out_shape=(rows, rows, wide, wide, tall), in_specs=[...]
where the time goes in v5:
time: 124 us; the launch traced here: 122 us
  Pallas kernels  121 us (98%)
    pallas_call x1, Pallas kernels, run_mega(): pl.pallas_call(mega, out_shape=(rows, rows, wide, wide, tall), in_specs=[...  116 us
    pallas_call x1, Pallas kernels, widen(): pl.pallas_call(widen_kernel, out_shape=(shape(block.shape, BF), shape(inn...  4.45 us

profile of v5, /device:TPU:0, one launch (start us, length us, event | category | flops | bytes accessed | tf_op | source)
XLA Modules:
  0.0 121.6 jit_solution(18082489414698050689)
XLA Ops:
  0.6 116.3 %mega.1 = (bf16[2,4,16,512]{3,2,1,0:T(8,128)(2,1)S(1)}, bf16[2,4,16,512]{3,2,1,0:T(8,128)(2,1)S(1)}, bf16[512,1920]{1,0:T(8,128)(2,1)S(1)}, bf16[512,1920]{1,0:T(8,128)(2,1)S(1)}, bf16[1920,512]{1,0:T(8,128)(2,1)S(1)}) custom-call(bf16[256,512]{1,0:T(8,128)(2,1)} %acts_hbm.1, bf16[256,512]{1,0:T(8,128)(2,1)} %grads_hbm.1, s32[1,16]{1,0:T(1,128)} %lengths_ref.1, ...), custom_call_target="tpu_custom_call" | custom-call | tf_op jit(solution)/shard_map/mega/pallas_call | solution.py:503
  117.0 4.4 %widen.1 = (bf16[128,512]{1,0:T(8,128)(2,1)}, bf16[128,512]{1,0:T(8,128)(2,1)}, f32[512,1920]{1,0:T(8,128)}, f32[512,1920]{1,0:T(8,128)}, f32[1920,512]{1,0:T(8,128)}) custom-call(bf16[128,512]{1,0:T(8,128)(2,1)S(1)} %bitcast.3, bf16[128,512]{1,0:T(8,128)(2,1)S(1)} %bitcast.4, bf16[512,1920]{1,0:T(8,128)(2,1)S(1)} %get-tuple-element.12.wide_a, ...), custom_call_target="tpu_custom_call" | custom-call | tf_op jit(solution)/shard_map/widen/pallas_call | solution.py:563

commit v6 on v5

--- a/solution.py
+++ b/solution.py
@@ -10,8 +10,8 @@
 WIDTH = 512
 HID = 1920
 PARTS = (1024, 896)
-YCOLS = (1792, 1664, 1792, 1664, 1280, 896, 1792, 1408)
-ACOLS = (1792, 2176, 1536, 1664, 1792, 1152, 1024, 2432)
+YCOLS = (1792, 1152, 1792, 1664, 1792, 1152, 1792, 896)
+ACOLS = (1792, 1664, 2304, 1152, 2048, 1664, 1024, 2176)
 NP = len(PARTS)
 NK = NS * NP
 BASES = tuple(sum(PARTS[:j]) for j in range(NP))
@@ -25,14 +25,14 @@
 TN = (((0,), (0,)), ((), ()))
 
 ORDER = (
-    0, 10, 20, 30, 40, 70, 80, 71, 81, 50, 100, 90, 72, 82, 110, 73, 83, 120, 111, 74, 60, 84, 101, 130,
-    140, 112, 102, 91, 131, 141, 103, 92, 93, 104, 113, 94, 132, 150, 121, 142, 122, 75, 114, 85, 180, 123,
-    124, 133, 143, 190, 151, 170, 152, 160, 220, 105, 134, 144, 95, 210, 115, 171, 191, 153, 161, 172, 221,
-    181, 200, 162, 154, 182, 192, 222, 125, 135, 145, 173, 193, 183, 163, 201, 223, 211, 202, 230, 174, 194,
-    212, 164, 184, 224, 240, 213, 155, 231, 76, 232, 203, 86, 214, 77, 204, 185, 87, 241, 233, 175, 165,
-    106, 195, 225, 96, 242, 116, 234, 107, 97, 243, 205, 215, 244, 117, 126, 136, 146, 127, 235, 137, 147,
-    156, 157, 245, 186, 196, 166, 176, 226, 187, 177, 167, 216, 197, 227, 206, 217, 207, 250, 236, 237, 246,
-    247, 260, 270,
+    0, 10, 20, 30, 40, 70, 80, 71, 50, 90, 100, 81, 72, 101, 91, 82, 110, 73, 120, 102, 92, 83, 74, 60, 130,
+    140, 121, 111, 103, 93, 84, 75, 122, 112, 94, 104, 85, 150, 131, 141, 113, 123, 95, 105, 132, 142, 114,
+    124, 190, 160, 170, 220, 151, 133, 143, 125, 152, 180, 134, 144, 115, 200, 171, 191, 161, 221, 153, 172,
+    192, 162, 210, 181, 222, 145, 154, 135, 182, 173, 201, 193, 230, 163, 211, 183, 223, 240, 202, 174, 184,
+    212, 194, 164, 224, 155, 231, 213, 76, 203, 214, 86, 77, 232, 185, 87, 241, 233, 204, 195, 175, 165,
+    106, 225, 242, 96, 116, 97, 107, 243, 215, 205, 117, 234, 126, 136, 146, 127, 235, 137, 147, 244, 156,
+    157, 245, 186, 196, 166, 176, 226, 187, 167, 197, 177, 216, 227, 206, 217, 207, 250, 236, 237, 246, 247,
+    260, 270,
 )
 
 SEQ_NAMES = (

time: 124 us -> 124 us (level)
  no operation moved by 1% of the time
where the time goes in v6:
time: 124 us; the launch traced here: 122 us
  Pallas kernels  121 us (98%)
    pallas_call x1, Pallas kernels, run_mega(): pl.pallas_call(mega, out_shape=(rows, rows, wide, wide, tall), in_specs=[...  117 us
    pallas_call x1, Pallas kernels, widen(): pl.pallas_call(widen_kernel, out_shape=(shape(block.shape, BF), shape(inn...  4.45 us

profile of v6, /device:TPU:0, one launch (start us, length us, event | category | flops | bytes accessed | tf_op | source)
XLA Modules:
  0.0 122.0 jit_solution(7323141133620286939)
XLA Ops:
  0.6 116.7 %mega.1 = (bf16[2,4,16,512]{3,2,1,0:T(8,128)(2,1)S(1)}, bf16[2,4,16,512]{3,2,1,0:T(8,128)(2,1)S(1)}, bf16[512,1920]{1,0:T(8,128)(2,1)S(1)}, bf16[512,1920]{1,0:T(8,128)(2,1)S(1)}, bf16[1920,512]{1,0:T(8,128)(2,1)S(1)}) custom-call(bf16[256,512]{1,0:T(8,128)(2,1)} %acts_hbm.1, bf16[256,512]{1,0:T(8,128)(2,1)} %grads_hbm.1, s32[1,16]{1,0:T(1,128)} %lengths_ref.1, ...), custom_call_target="tpu_custom_call" | custom-call | tf_op jit(solution)/shard_map/mega/pallas_call | solution.py:503
  117.4 4.4 %widen.1 = (bf16[128,512]{1,0:T(8,128)(2,1)}, bf16[128,512]{1,0:T(8,128)(2,1)}, f32[512,1920]{1,0:T(8,128)}, f32[512,1920]{1,0:T(8,128)}, f32[1920,512]{1,0:T(8,128)}) custom-call(bf16[128,512]{1,0:T(8,128)(2,1)S(1)} %bitcast.3, bf16[128,512]{1,0:T(8,128)(2,1)S(1)} %bitcast.4, bf16[512,1920]{1,0:T(8,128)(2,1)S(1)} %get-tuple-element.12.wide_a, ...), custom_call_target="tpu_custom_call" | custom-call | tf_op jit(solution)/shard_map/widen/pallas_call | solution.py:563
